TPU v7x, 256 devices: a whole 4x4x8 slice. The times are simulated.
256 devices in a mesh: row: 32 (over y, x, core), col: 8 (over z).
Axes of the slice: x: 4, y: 4, z: 8, core: 2. Of those that a mesh axis runs over, the one named last changes fastest.
Arguments:
- features: bfloat16 [524288, 256], P(('row', 'col')), may hold values from -6 to 6
- w_self: bfloat16 [256, 256], replicated, may hold values from -0.375 to 0.375
- w_neigh: bfloat16 [256, 256], replicated, may hold values from -1.5 to 1.5
- bias: float32 [256], replicated, may hold values from -3 to 3
- hub_ids: int32 [6], replicated, may hold values from 0 to 31
- hub_adj: bfloat16 [256, 6, 2048, 256], P(('row', 'col')), may hold values from 0 to 2, as said below
- send_tile: int32 [256, 8, 2], P(('row', 'col')), may hold values from 0 to 15
- recv_count: int32 [256, 8], P(('row', 'col')), may hold values from 0 to 2, as said below
- recv_dst: int32 [256, 8, 2], P(('row', 'col')), may hold values from 0 to 15
- recv_adj: bfloat16 [256, 8, 2, 128, 128], P(('row', 'col')), may hold values from 0 to 2, as said below
- cotangent: bfloat16 [524288, 256], P(('row', 'col')), may hold values from -6 to 6
Outputs:
- output: bfloat16 [524288, 256], P(('row', 'col'))
- feature_grad: bfloat16 [524288, 256], P(('row', 'col'))
Inputs may be any that keep to these rules, and one draw needn't show every extreme that they name: `recv_count`: every device uses all 2 slots from at least one device of its row group. `hub_adj`: nonnegative edge weights. `recv_adj`: nonnegative edge weights.
All inputs are finite; a program needn't handle non-finite values.
Results may differ from a plain program's by a relative error of at most 0.0055.
Values may be sent and summed in bfloat16 or wider, within the bound.
A program may use at most 64 MiB of HBM per device.

v0:
```python
import jax
import jax.numpy as jnp
from jax import lax
from jax.sharding import PartitionSpec as P


def from_root(value, axis, source):
    kept = jnp.where(lax.axis_index(axis) == source, value, 0).astype(value.dtype)
    return lax.psum(kept, axis)


def shards(
    features,
    w_self,
    w_neigh,
    bias,
    hub_ids,
    hub_adj,
    send_tile,
    recv_count,
    recv_dst,
    recv_adj,
    cotangent,
):
    f32 = jnp.float32
    bf16 = jnp.bfloat16
    nodes, width = features.shape
    sections = hub_ids.shape[0]
    hub_rows = hub_adj.shape[3]
    peers, slots, tile = (recv_adj.shape[1], recv_adj.shape[2], recv_adj.shape[3])
    total = peers * slots
    count_tiles = nodes // tile
    row_pos = lax.axis_index("row")
    adjacency = hub_adj[0]
    own_hub = features[:hub_rows]
    hub_sum = jnp.zeros((nodes, width), f32)
    for section in range(sections):
        owner = hub_ids[section]
        block = from_root(own_hub, "row", owner)
        hub_sum = hub_sum + jnp.dot(adjacency[section], block, preferred_element_type=f32)
    offered = send_tile[0].reshape(total)
    outgoing = features.reshape(count_tiles, tile, width)[offered].reshape(
        peers, slots, tile, width
    )
    incoming = lax.all_to_all(outgoing, "col", split_axis=0, concat_axis=0, tiled=True)
    live = (
        (jnp.arange(slots, dtype=jnp.int32)[None, :] < recv_count[0][:, None])
        .astype(f32)
        .reshape(total)
    )
    landing = recv_dst[0].reshape(total)
    select = (landing[:, None] == jnp.arange(count_tiles, dtype=jnp.int32)[None, :]).astype(
        f32
    ) * live[:, None]
    weights = recv_adj[0].reshape(total, tile, tile)
    contrib = jnp.einsum(
        "sij,sjd->sid", weights, incoming.reshape(total, tile, width), preferred_element_type=f32
    )
    tile_sum = jnp.einsum("sn,sid->nid", select, contrib, precision=lax.Precision.HIGHEST).reshape(
        nodes, width
    )
    row_weight = jnp.sum(weights.astype(f32), axis=2)
    tile_deg = jnp.einsum("sn,si->ni", select, row_weight, precision=lax.Precision.HIGHEST).reshape(
        nodes
    )
    degree = 1.0 + jnp.sum(adjacency.astype(f32), axis=(0, 2)) + tile_deg
    agg = ((tile_sum + hub_sum) / degree[:, None]).astype(bf16)
    pre = (
        jnp.dot(features, w_self, preferred_element_type=f32)
        + jnp.dot(agg, w_neigh, preferred_element_type=f32)
        + bias
    )
    sig = jax.nn.sigmoid(pre)
    output = (pre * sig).astype(bf16)
    grad = (cotangent.astype(f32) * sig * (1.0 + pre * (1.0 - sig))).astype(bf16)
    contract = (((1,), (1,)), ((), ()))
    self_grad = lax.dot_general(grad, w_self, contract, preferred_element_type=f32)
    agg_grad = (
        lax.dot_general(grad, w_neigh, contract, preferred_element_type=f32) / degree[:, None]
    ).astype(bf16)
    hub_back = jnp.zeros((hub_rows, width), f32)
    for section in range(sections):
        partial_grad = lax.dot_general(
            adjacency[section], agg_grad, (((0,), (0,)), ((), ())), preferred_element_type=f32
        )
        summed_section = lax.psum(partial_grad, "row")
        hub_back = hub_back + jnp.where(row_pos == hub_ids[section], summed_section, 0.0)
    dest_rows = agg_grad.reshape(count_tiles, tile, width)[landing]
    slot_grad = (
        jnp.einsum("sij,sid->sjd", weights, dest_rows, preferred_element_type=f32)
        * live[:, None, None]
    ).astype(bf16)
    returned = lax.all_to_all(
        slot_grad.reshape(peers, slots, tile, width), "col", split_axis=0, concat_axis=0, tiled=True
    )
    owned = (offered[:, None] == jnp.arange(count_tiles, dtype=jnp.int32)[None, :]).astype(f32)
    tile_back = jnp.einsum(
        "sn,sid->nid",
        owned,
        returned.reshape(total, tile, width).astype(f32),
        precision=lax.Precision.HIGHEST,
    ).reshape(nodes, width)
    hub_padded = jnp.concatenate([hub_back, jnp.zeros((nodes - hub_rows, width), f32)], axis=0)
    feature_grad = (self_grad + tile_back + hub_padded).astype(bf16)
    return (output, feature_grad)


def solution(mesh):
    placed = (
        P(("row", "col"), None),
        P(),
        P(),
        P(),
        P(),
        P(("row", "col"), None, None, None),
        P(("row", "col"), None, None),
        P(("row", "col"), None),
        P(("row", "col"), None, None),
        P(("row", "col"), None, None, None, None),
        P(("row", "col"), None),
    )
    return jax.shard_map(
        shards,
        mesh=mesh,
        in_specs=placed,
        out_specs=(P(("row", "col"), None), P(("row", "col"), None)),
        check_vma=False,
    )
```

profile of v0, /device:TPU:1, one launch (start us, length us, event | category | flops | bytes accessed | tf_op | source)
XLA Modules:
  0.0 319.7 jit_solution(17392515614874184246)
XLA Ops:
  7.2 0.8 copy.26
  8.0 0.1 reshape_squeeze.9
  8.1 2.9 gather_fusion
  11.0 9.1 %all-to-all-start = ((bf16[8,2,128,256]{3,2,1,0:T(8,128)(2,1)}), bf16[8,2,128,256]{3,2,1,0:T(8,128)(2,1)}, u32[]{:S(2)}, u32[]{:S(2)}) async-start(bf16[8,2,128,256]{3,2,1,0:T(8,128)(2,1)} %bitcast.4), calls=%async_computation | async-start | bytes 2097152 | tf_op jit(solution)/shard_map/all_to_all | solution.py:45
  20.1 0.0 all-reduce.8.cloned.1.call-start
  20.2 0.7 fusion.55
  24.8 0.9 broadcast_select_fusion
  25.7 0.1 copy.25
  25.8 0.1 eq.54
  25.9 0.1 reshape_squeeze.11
  26.0 0.1 fusion.50
  26.0 0.1 reshape.153
  26.1 0.2 convert_reduce_fusion.1
  26.4 3.7 %convert_reduce_fusion = f32[2048]{0:T(1024)S(1)} fusion(bf16[1,6,2048,256]{3,2,1,0:T(8,128)(2,1)} %param.16), kind=kLoop, calls=%fused_computation.2 | loop fusion | flops 6289408 | bytes 6299648 | tf_op jit(solution)/shard_map/reduce_sum | solution.py:66
  30.1 0.1 fusion.10
  30.2 1.8 fusion.58
  32.0 111.3 %all-reduce.8.cloned.1.call-done = (bf16[256,256]{1,0:T(8,128)(2,1)}, bf16[256,256]{1,0:T(8,128)(2,1)}, bf16[256,256]{1,0:T(8,128)(2,1)}, bf16[256,256]{1,0:T(8,...) async-done(((bf16[256,256]{1,0:T(8,128)(2,1)}, bf16[256,256]{1,0:T(8,128)(2,1)}, bf16[256,256]{1,0:T(8,128)(2,1)}, bf16[256,256]{1,0:T(8,128)(2,1)}, ...) | async-done | bytes 786448 | tf_op jit(solution)/shard_map/psum | solution.py:9
  143.3 1.8 fusion.23
  145.1 1.7 convolution_add_fusion.4
  146.8 0.4 convolution_add_fusion.3
  147.3 0.5 copy-done.8
  147.7 0.4 convolution_add_fusion.2
  148.2 0.5 copy-done.7
  148.6 1.7 convolution_add_fusion.1
  150.4 3.1 fusion.59
  153.5 2.2 copy.39
  155.7 1.9 fusion.8
  157.6 2.6 copy.27
  160.2 5.6 %multiply_convert_fusion.1 = (bf16[2048,256]{1,0:T(8,128)(2,1)}, bf16[2048,256]{1,0:T(8,128)(2,1)}) fusion(bf16[2048,256]{1,0:T(8,128)(2,1)} %param.21, f32[256]{0:T(256)S(1)} %copy-done.15, f32[2048,256]{1,0:T(8,128)S(1)} %copy-done.4, bf16[256,256]{1,0:T(8,128)(2,1)S(1)} %copy-done, f32[2048,256]{1,0:T(8,128)} %bitcast.125, ...), kind=kOutput, calls=%fused_computation.22 | convolution fusion | flops 546308096 | bytes 10757120 | tf_op jit(solution)/shard_map/dot_general | solution.py:70
  165.8 1.7 fusion.5
  167.5 2.4 convolution_bitcast_fusion
  170.0 2.4 convolution_bitcast_fusion.1
  172.4 2.5 convolution_bitcast_fusion.2
  174.8 0.6 gather_fusion.1
  175.5 1.5 multiply_convert_fusion
  177.0 6.8 %all-to-all-start.1 = ((bf16[8,2,128,256]{2,3,1,0:T(8,128)(2,1)}), bf16[8,2,128,256]{2,3,1,0:T(8,128)(2,1)S(1)}, u32[]{:S(2)}, u32[]{:S(2)}) async-start(bf16[8,2,128,256]{2,3,1,0:T(8,128)(2,1)} %bitcast.28), calls=%async_computation.1 | async-start | bytes 2097152 | tf_op jit(solution)/shard_map/all_to_all | solution.py:93
  183.8 0.2 all-reduce.6.cloned.1.call-start
  184.0 2.5 convolution_bitcast_fusion.3
  186.5 2.4 convolution_bitcast_fusion.4
  188.9 2.4 convolution_bitcast_fusion.5
  191.3 0.0 all-reduce.6.cloned.1.call-update
  191.4 0.1 eq.64
  191.4 117.2 %all-reduce.6.cloned.1.call-done = (f32[256,256]{1,0:T(8,128)}, f32[256,256]{1,0:T(8,128)}, f32[256,256]{1,0:T(8,128)}, f32[256,256]{1,0:T(8,128)}, f32[256,256]{1,0:T(8,128)}, /*index=5*/f32[256,256]{1,0:T(8,128)}) async-done(((f32[256,256]{1,0:T(8,128)}, f32[256,256]{1,0:T(8,128)}, f32[256,256]{1,0:T(8,128)}, f32[256,256]{1,0:T(8,128)}, f32[256,256]{1,0:T(8,128)}, /*index=5*/f32[256,256]{1,0:T(8,128)}), ...) | async-done | bytes 1572880 | tf_op jit(solution)/shard_map/psum | solution.py:86
  308.7 0.1 select_add_fusion
  308.8 0.9 copy.47
  309.7 0.4 fusion.41
  310.1 1.2 copy.32
  311.4 1.5 fusion.4
  (42 shorter events, 0.1 us)
Async XLA Ops:
  7.2 153.0 %copy-start = (bf16[256,256]{1,0:T(8,128)(2,1)S(1)}, bf16[256,256]{1,0:T(8,128)(2,1)}, u32[]{:S(2)}) copy-start(bf16[256,256]{1,0:T(8,128)(2,1)} %param.13) | copy-start | bytes 393220
  8.1 12.1 %copy-start.11 = (s32[6]{0:T(128)S(1)}, s32[6]{0:T(128)}, u32[]{:S(2)}) copy-start(s32[6]{0:T(128)} %param.15) | copy-start | bytes 76
  8.1 16.7 %copy-start.1 = (bf16[2048,256]{1,0:T(8,128)(2,1)S(1)}, bf16[2048,256]{1,0:T(8,128)(2,1)}, u32[]{:S(2)}) copy-start(bf16[2048,256]{1,0:T(8,128)(2,1)} %param.11) | copy-start | bytes 3145732
  11.0 14.7 %copy-start.12 = (s32[1,8,2]{1,2,0:T(2,128)S(1)}, s32[1,8,2]{1,2,0:T(2,128)}, u32[]{:S(2)}) copy-start(s32[1,8,2]{1,2,0:T(2,128)} %param.19) | copy-start | bytes 196
  11.0 15.0 %copy-start.13 = (s32[1,8]{1,0:T(1,128)S(1)}, s32[1,8]{1,0:T(1,128)}, u32[]{:S(2)}) copy-start(s32[1,8]{1,0:T(1,128)} %param.18) | copy-start | bytes 100
  11.0 15.1 %copy-start.2 = (bf16[1,8,2,128,128]{4,3,2,1,0:T(8,128)(2,1)S(1)}, bf16[1,8,2,128,128]{4,3,2,1,0:T(8,128)(2,1)}, u32[]{:S(2)}) copy-start(bf16[1,8,2,128,128]{4,3,2,1,0:T(8,128)(2,1)} %param.20) | copy-start | bytes 1572868
  11.0 139.4 %all-to-all-start = ((bf16[8,2,128,256]{3,2,1,0:T(8,128)(2,1)}), bf16[8,2,128,256]{3,2,1,0:T(8,128)(2,1)}, u32[]{:S(2)}, u32[]{:S(2)}) async-start(bf16[8,2,128,256]{3,2,1,0:T(8,128)(2,1)} %bitcast.4), calls=%async_computation | async-start | bytes 2097152 | tf_op jit(solution)/shard_map/all_to_all | solution.py:45
  20.1 123.1 %all-reduce.8.cloned.1.call-start = ((), (), s32[]{:S(2)}) async-start(), calls=%async_computation.3 | async-start | bytes 1572864 | tf_op jit(solution)/shard_map/psum | solution.py:9
  26.4 3.9 %copy-start.6 = (bf16[256,256]{1,0:T(8,128)(2,1)S(1)}, bf16[256,256]{1,0:T(8,128)(2,1)}, u32[]{:S(2)}) copy-start(bf16[256,256]{1,0:T(8,128)(2,1)} %param.12) | copy-start | bytes 393220
  30.2 116.6 %slice-start = ((s8[6291456]{0:T(1024)(128)(4,1)}), s8[2097152]{0:T(1024)(128)(4,1)S(1)}, s32[]{:S(2)}) async-start(s8[6291456]{0:T(1024)(128)(4,1)} %bitcast.118), calls=%async_computation.4 | async-start | bytes 4194304
  143.3 1.8 copy-start.10
  143.3 3.5 %slice-start.1 = ((s8[6291456]{0:T(1024)(128)(4,1)}), s8[4194304]{0:T(1024)(128)(4,1)S(1)}, s32[]{:S(2)}) async-start(s8[6291456]{0:T(1024)(128)(4,1)} %bitcast.118), calls=%async_computation.5 | async-start | bytes 8388608
  145.1 1.7 copy-start.9
  146.8 0.9 copy-start.8
  147.7 0.9 copy-start.7
  148.6 1.8 copy-start.3
  157.6 2.6 copy-start.4
  157.6 2.6 copy-start.14
  157.6 2.6 copy-start.15
  177.0 131.8 %all-to-all-start.1 = ((bf16[8,2,128,256]{2,3,1,0:T(8,128)(2,1)}), bf16[8,2,128,256]{2,3,1,0:T(8,128)(2,1)S(1)}, u32[]{:S(2)}, u32[]{:S(2)}) async-start(bf16[8,2,128,256]{2,3,1,0:T(8,128)(2,1)} %bitcast.28), calls=%async_computation.1 | async-start | bytes 2097152 | tf_op jit(solution)/shard_map/all_to_all | solution.py:93
  183.8 124.9 %all-reduce.6.cloned.1.call-start = ((), (), s32[]{:S(2)}) async-start(), calls=%async_computation.2 | async-start | bytes 3145728 | tf_op jit(solution)/shard_map/psum | solution.py:86
  310.1 1.2 copy-start.5
Sparse Core Ops, SparseCore 0:
  25.8 117.4 all-reduce.7
  191.5 117.1 all-reduce.5
where the time goes:
time: 320 us
  waiting for transfers between devices  229 us (72%)
  matrix products  38.3 us (12%)
  between operations  18.2 us (6%)
  starting transfers between devices  16.2 us (5%)
  local copies, waits for them, and re-layouts  13.4 us (4%)
  other arithmetic  5.03 us (2%)
    psum x1, waiting for transfers between devices, shards(): summed_section = lax.psum(partial_grad, 'row')  117 us
    psum x1, waiting for transfers between devices, from_root(): return lax.psum(kept, axis)  111 us
    dot_general x6, matrix products, shards(): lax.dot_general(adjacency[section], agg_grad, (((0,), (0,)), ((), ())), p...  14.7 us
    all_to_all x1, starting transfers between devices, shards(): lax.all_to_all(outgoing, 'col', split_axis=0, concat_axis=0, tiled=True)  9.15 us
    all_to_all x1, starting transfers between devices, shards(): lax.all_to_all(slot_grad.reshape(peers, slots, tile, width), 'col', split...  6.76 us
  transfers between devices with their start and end apart: 4, of which 2 were waited for; matrix products, arithmetic and copies ran while one was open for 7% of the time, Pallas kernels for 0%

commit v1 on v0

--- a/solution.py
+++ b/solution.py
@@ -2,11 +2,6 @@
 import jax.numpy as jnp
 from jax import lax
 from jax.sharding import PartitionSpec as P
-
-
-def from_root(value, axis, source):
-    kept = jnp.where(lax.axis_index(axis) == source, value, 0).astype(value.dtype)
-    return lax.psum(kept, axis)
 
 
 def shards(
@@ -30,18 +25,24 @@
     peers, slots, tile = (recv_adj.shape[1], recv_adj.shape[2], recv_adj.shape[3])
     total = peers * slots
     count_tiles = nodes // tile
-    row_pos = lax.axis_index("row")
     adjacency = hub_adj[0]
-    own_hub = features[:hub_rows]
+    rows_n = lax.axis_size("row")
+    part = hub_rows // rows_n
+    pieces = lax.all_to_all(
+        features[:hub_rows].reshape(rows_n, part, width), "row", split_axis=0, concat_axis=0, tiled=True
+    )
+    picked = jnp.stack(
+        [lax.dynamic_index_in_dim(pieces, hub_ids[s], 0, keepdims=False) for s in range(sections)]
+    )
+    gathered = lax.all_gather(picked, "row", axis=0, tiled=False)
+    blocks = jnp.transpose(gathered, (1, 0, 2, 3)).reshape(sections, hub_rows, width)
     hub_sum = jnp.zeros((nodes, width), f32)
     for section in range(sections):
-        owner = hub_ids[section]
-        block = from_root(own_hub, "row", owner)
-        hub_sum = hub_sum + jnp.dot(adjacency[section], block, preferred_element_type=f32)
+        hub_sum = hub_sum + jnp.dot(adjacency[section], blocks[section], preferred_element_type=f32)
     offered = send_tile[0].reshape(total)
-    outgoing = features.reshape(count_tiles, tile, width)[offered].reshape(
-        peers, slots, tile, width
-    )
+    outgoing = jnp.stack(
+        [lax.dynamic_slice_in_dim(features, offered[i] * tile, tile, 0) for i in range(total)]
+    ).reshape(peers, slots, tile, width)
     incoming = lax.all_to_all(outgoing, "col", split_axis=0, concat_axis=0, tiled=True)
     live = (
         (jnp.arange(slots, dtype=jnp.int32)[None, :] < recv_count[0][:, None])
@@ -78,14 +79,26 @@
     agg_grad = (
         lax.dot_general(grad, w_neigh, contract, preferred_element_type=f32) / degree[:, None]
     ).astype(bf16)
-    hub_back = jnp.zeros((hub_rows, width), f32)
-    for section in range(sections):
-        partial_grad = lax.dot_general(
-            adjacency[section], agg_grad, (((0,), (0,)), ((), ())), preferred_element_type=f32
-        )
-        summed_section = lax.psum(partial_grad, "row")
-        hub_back = hub_back + jnp.where(row_pos == hub_ids[section], summed_section, 0.0)
-    dest_rows = agg_grad.reshape(count_tiles, tile, width)[landing]
+    partials = jnp.stack(
+        [
+            lax.dot_general(
+                adjacency[section], agg_grad, (((0,), (0,)), ((), ())), preferred_element_type=f32
+            ).astype(bf16)
+            for section in range(sections)
+        ]
+    ).reshape(sections, rows_n, part, width)
+    landed = lax.all_to_all(partials, "row", split_axis=1, concat_axis=1, tiled=True)
+    summed = jnp.sum(landed.astype(f32), axis=1)
+    owners = (hub_ids[None, :] == jnp.arange(rows_n, dtype=jnp.int32)[:, None]).astype(f32)
+    to_owner = jnp.sum(owners[:, :, None, None] * summed[None], axis=1).astype(bf16)
+    hub_back = (
+        lax.all_to_all(to_owner, "row", split_axis=0, concat_axis=0, tiled=True)
+        .astype(f32)
+        .reshape(hub_rows, width)
+    )
+    dest_rows = jnp.stack(
+        [lax.dynamic_slice_in_dim(agg_grad, landing[i] * tile, tile, 0) for i in range(total)]
+    )
     slot_grad = (
         jnp.einsum("sij,sid->sjd", weights, dest_rows, preferred_element_type=f32)
         * live[:, None, None]

time: 320 us -> 206 us (0.64)
  waiting for transfers between devices: 229 us -> 42.1 us
  blocking collectives: 0 us -> 25.5 us
  starting transfers between devices: 16.2 us -> 33.4 us
  between operations: 18.2 us -> 32.4 us
  local copies, waits for them, and re-layouts: 13.4 us -> 27.4 us
    psum x2 -> x0, waiting for transfers between devices: 228 us -> none  [the longest x1 117 us: shards(): summed_section = lax.psum(partial_grad, 'row')]
    all_to_all x1, waiting for transfers between devices: 0.01 us -> 28.2 us  [shards(): lax.all_to_all(slot_grad.reshape(peers, slots, tile, width), 'col', split...]
    all_gather x0 -> x1, blocking collectives: none -> 25.5 us  [shards(): gathered = lax.all_gather(picked, 'row', axis=0, tiled=False)]
    all_to_all x0 -> x3, starting transfers between devices: none -> 18.2 us  [the longest x1 8.59 us: shards(): lax.all_to_all(features[:hub_rows].reshape(rows_n, part, width), 'row', s...]
    all_to_all x0 -> x3, waiting for transfers between devices: none -> 13.9 us  [the longest x1 8.89 us: shards(): lax.all_to_all(partials, 'row', split_axis=1, concat_axis=1, tiled=True)]
    unnamed x38 -> x69, local copies, waits for them, and re-layouts: 1.87 us -> 13.7 us
    reshape x0 -> x3, local copies, waits for them, and re-layouts: none -> 4.82 us  [the longest x1 1.85 us: shards(): jnp.einsum('sn,sid->nid', select, contrib, precision=lax.Precision.HIGHEST)]
    gather x2 -> x0, local copies, waits for them, and re-layouts: 3.51 us -> none  [the longest x1 2.89 us: shards(): features.reshape(count_tiles, tile, width)[offered]]
  transfers between devices with their start and end apart: 4 -> 5, of which waited for: 2 -> 3; matrix products, arithmetic and copies ran while one was open for 7% -> 17% of each run, Pallas kernels for 0% -> 0%
where the time goes in v1:
time: 206 us; the launch traced here: 204 us
  waiting for transfers between devices  42.1 us (20%)
  matrix products  38.4 us (19%)
  starting transfers between devices  33.4 us (16%)
  between operations  32.4 us (16%)
  local copies, waits for them, and re-layouts  27.4 us (13%)
  blocking collectives  25.5 us (12%)
  other arithmetic  5.07 us (2%)
    all_to_all x1, waiting for transfers between devices, shards(): lax.all_to_all(slot_grad.reshape(peers, slots, tile, width), 'col', split...  28.2 us
    all_gather x1, blocking collectives, shards(): gathered = lax.all_gather(picked, 'row', axis=0, tiled=False)  25.5 us
    dot_general x6, matrix products, shards(): lax.dot_general(adjacency[section], agg_grad, (((0,), (0,)), ((), ())), p...  14.8 us
    unnamed x69, local copies, waits for them, and re-layouts  13.7 us
    all_to_all x1, waiting for transfers between devices, shards(): lax.all_to_all(partials, 'row', split_axis=1, concat_axis=1, tiled=True)  8.89 us
    all_to_all x1, starting transfers between devices, shards(): lax.all_to_all(features[:hub_rows].reshape(rows_n, part, width), 'row', s...  8.59 us
    all_to_all x1, starting transfers between devices, shards(): lax.all_to_all(outgoing, 'col', split_axis=0, concat_axis=0, tiled=True)  8.33 us
    all_to_all x1, starting transfers between devices, shards(): lax.all_to_all(slot_grad.reshape(peers, slots, tile, width), 'col', split...  6.92 us
  transfers between devices with their start and end apart: 5, of which 3 were waited for; matrix products, arithmetic and copies ran while one was open for 17% of the time, Pallas kernels for 0%

profile of v1, /device:TPU:1, one launch (start us, length us, event | category | flops | bytes accessed | tf_op | source)
XLA Modules:
  0.0 204.4 jit_solution(7526366855033646529)
XLA Ops:
  0.7 1.7 slice_bitcast_fusion.13
  2.3 8.6 %all-to-all-start.1 = ((bf16[32,8,256]{2,1,0:T(8,128)(2,1)}), bf16[32,8,256]{2,1,0:T(8,128)(2,1)S(1)}, u32[]{:S(2)}, u32[]{:S(2)}) async-start(bf16[32,8,256]{2,1,0:T(8,128)(2,1)} %slice_bitcast_fusion.13), calls=%async_computation.1 | async-start | bytes 262144 | tf_op jit(solution)/shard_map/all_to_all | solution.py:31
  10.9 0.8 copy.132
  22.6 1.6 fusion.66
  43.1 0.9 constant_dynamic-update-slice_fusion.15
  44.0 0.8 constant_dynamic-update-slice_fusion.14
  44.9 0.8 constant_dynamic-update-slice_fusion.13
  45.7 0.8 constant_dynamic-update-slice_fusion.12
  46.6 0.8 constant_dynamic-update-slice_fusion.11
  47.4 0.8 constant_dynamic-update-slice_fusion.10
  48.3 0.8 constant_dynamic-update-slice_fusion.9
  49.1 0.8 constant_dynamic-update-slice_fusion.8
  49.9 0.8 constant_dynamic-update-slice_fusion.7
  50.9 1.3 copy.133
  52.7 3.7 %convert_reduce_fusion = f32[2048]{0:T(1024)S(1)} fusion(bf16[1,6,2048,256]{3,2,1,0:T(8,128)(2,1)} %param.16), kind=kLoop, calls=%fused_computation | loop fusion | flops 6289408 | bytes 6299648 | tf_op jit(solution)/shard_map/reduce_sum | solution.py:67
  56.4 1.8 fusion.70
  62.2 8.3 %all-to-all-start = ((bf16[8,2,128,256]{2,3,1,0:T(8,128)(2,1)}), bf16[8,2,128,256]{2,3,1,0:T(8,128)(2,1)}, u32[]{:S(2)}, u32[]{:S(2)}) async-start(bf16[8,2,128,256]{2,3,1,0:T(8,128)(2,1)} %copy.133), calls=%async_computation | async-start | bytes 2097152 | tf_op jit(solution)/shard_map/all_to_all | solution.py:46
  70.6 25.5 %all-gather = bf16[192,8,256]{2,1,0:T(8,128)(2,1)S(1)} all-gather(bf16[6,8,256]{2,1,0:T(8,128)(2,1)S(1)} %constant_dynamic-update-slice_fusion.16), channel_id=2, replica_groups=mesh['row'=32,'col'=8] {'row'}, dimensions={0}, use_global_device_ids=true | all-gather | bytes 811008 | tf_op jit(solution)/shard_map/all_gather | solution.py:37
  96.1 1.9 fusion.33
  98.0 1.7 convolution_add_fusion.6
  100.8 1.8 convolution_add_fusion.3
  102.6 3.0 %convolution_bitcast_fusion = f32[16,128,256]{1,2,0:T(8,128)} fusion(bf16[16,128,256]{1,2,0:T(8,128)(2,1)} %bitcast.35, bf16[16,128,128]{2,1,0:T(8,128)(2,1)S(1)} %bitcast.269), kind=kOutput, calls=%fused_computation.21 | convolution fusion | flops 134217728 | bytes 3670016 | tf_op jit(solution)/shard_map/sij,sjd->sid/dot_general | solution.py:57
  105.6 2.2 %copy.134 = f32[16,128,256]{2,0,1:T(8,128)S(1)} copy(f32[16,128,256]{1,2,0:T(8,128)} %convolution_bitcast_fusion) | data formatting | bytes 4194304 | tf_op jit(solution)/shard_map/sij,sjd->sid/dot_general | solution.py:57
  107.9 2.5 %fusion.51 = f32[16,128,256]{2,0,1:T(8,128)S(1)} fusion(f32[16,128,256]{2,0,1:T(8,128)S(1)} %copy.134, f32[16]{0:T(128)} %copy-done.10, s32[16]{0:T(128)S(1)} %eq.45), kind=kOutput, calls=%fused_computation.126 | convolution fusion | flops 100663808 | bytes 4194432 | tf_op jit(solution)/shard_map/sn,sid->nid/dot_general | solution.py:60
  110.4 1.2 copy.135
  111.6 1.9 copy.136
  113.5 6.0 %multiply_convert_fusion.1 = (bf16[2048,256]{1,0:T(8,128)(2,1)S(1)}, bf16[2048,256]{1,0:T(8,128)(2,1)}) fusion(bf16[2048,256]{1,0:T(8,128)(2,1)} %param.21, f32[256]{0:T(256)S(1)} %copy-done.13, f32[2048,256]{1,0:T(8,128)} %fusion.70, bf16[256,256]{1,0:T(8,128)(2,1)S(1)} %copy-done, f32[2048,256]{0,1:T(8,128)} %copy.136, ...), kind=kOutput, calls=%fused_computation.18 | convolution fusion | flops 546308096 | bytes 10757120 | tf_op jit(solution)/shard_map/dot_general | solution.py:71
  120.4 2.8 %fusion.9 = bf16[6,32,8,256]{3,2,0,1:T(8,128)(2,1)} fusion(bf16[2048,256]{0,1:T(8,128)(2,1)S(1)} %fusion.5, bf16[1,6,2048,256]{3,2,1,0:T(8,128)(2,1)} %param.16), kind=kOutput, calls=%fused_computation.31 | convolution fusion | flops 268500992 | bytes 2228224 | tf_op jit(solution)/shard_map/dot_general | solution.py:84
  123.2 2.4 %fusion.11 = bf16[6,32,8,256]{3,2,0,1:T(8,128)(2,1)} fusion(bf16[6,32,8,256]{3,2,0,1:T(8,128)(2,1)} %fusion.9, bf16[2048,256]{0,1:T(8,128)(2,1)S(1)} %fusion.5, bf16[1,6,2048,256]{3,2,1,0:T(8,128)(2,1)} %param.16), kind=kOutput, calls=%fused_computation.33 | convolution fusion | flops 268500992 | bytes 2228224 | tf_op jit(solution)/shard_map/dot_general | solution.py:84
  125.6 2.4 %fusion.13 = bf16[6,32,8,256]{3,2,0,1:T(8,128)(2,1)} fusion(bf16[6,32,8,256]{3,2,0,1:T(8,128)(2,1)} %fusion.11, bf16[2048,256]{0,1:T(8,128)(2,1)S(1)} %fusion.5, bf16[1,6,2048,256]{3,2,1,0:T(8,128)(2,1)} %param.16), kind=kOutput, calls=%fused_computation.35 | convolution fusion | flops 268500992 | bytes 2228224 | tf_op jit(solution)/shard_map/dot_general | solution.py:84
  128.1 2.4 %fusion.15 = bf16[6,32,8,256]{3,2,0,1:T(8,128)(2,1)} fusion(bf16[6,32,8,256]{3,2,0,1:T(8,128)(2,1)} %fusion.13, bf16[2048,256]{0,1:T(8,128)(2,1)S(1)} %fusion.5, bf16[1,6,2048,256]{3,2,1,0:T(8,128)(2,1)} %param.16), kind=kOutput, calls=%fused_computation.37 | convolution fusion | flops 268500992 | bytes 2228224 | tf_op jit(solution)/shard_map/dot_general | solution.py:84
  130.5 2.4 %fusion.17 = bf16[6,32,8,256]{3,2,0,1:T(8,128)(2,1)} fusion(bf16[6,32,8,256]{3,2,0,1:T(8,128)(2,1)} %fusion.15, bf16[2048,256]{0,1:T(8,128)(2,1)S(1)} %fusion.5, bf16[1,6,2048,256]{3,2,1,0:T(8,128)(2,1)} %param.16), kind=kOutput, calls=%fused_computation.39 | convolution fusion | flops 268500992 | bytes 2228224 | tf_op jit(solution)/shard_map/dot_general | solution.py:84
  132.9 2.4 %fusion.19 = bf16[6,32,8,256]{3,2,0,1:T(8,128)(2,1)} fusion(bf16[6,32,8,256]{3,2,0,1:T(8,128)(2,1)} %fusion.17, bf16[2048,256]{0,1:T(8,128)(2,1)S(1)} %fusion.5, bf16[1,6,2048,256]{3,2,1,0:T(8,128)(2,1)} %param.16), kind=kOutput, calls=%fused_computation.41 | convolution fusion | flops 268500992 | bytes 2228224 | tf_op jit(solution)/shard_map/dot_general | solution.py:84
  135.3 5.2 %all-to-all-start.3 = ((bf16[6,32,8,256]{3,2,0,1:T(8,128)(2,1)}), bf16[6,32,8,256]{3,2,0,1:T(8,128)(2,1)S(1)}, u32[]{:S(2)}, u32[]{:S(2)}) async-start(bf16[6,32,8,256]{3,2,0,1:T(8,128)(2,1)} %fusion.19), calls=%async_computation.3 | async-start | bytes 1572864 | tf_op jit(solution)/shard_map/all_to_all | solution.py:90
  140.6 0.9 constant_dynamic-update-slice_fusion.37
  141.4 0.9 constant_dynamic-update-slice_fusion.36
  142.3 0.9 constant_dynamic-update-slice_fusion.35
  143.1 0.9 constant_dynamic-update-slice_fusion.34
  144.5 1.4 multiply_convert_fusion
  145.9 8.9 %all-to-all-done.3 = bf16[6,32,8,256]{3,2,0,1:T(8,128)(2,1)S(1)} async-done(((bf16[6,32,8,256]{3,2,0,1:T(8,128)(2,1)}), bf16[6,32,8,256]{3,2,0,1:T(8,128)(2,1)S(1)}, u32[]{:S(2)}, u32[]{:S(2)}) %all-to-all-start.3) | async-done | bytes 786464 | tf_op jit(solution)/shard_map/all_to_all | solution.py:90
  154.8 6.9 %all-to-all-start.2 = ((bf16[8,2,128,256]{2,3,1,0:T(8,128)(2,1)}), bf16[8,2,128,256]{2,3,1,0:T(8,128)(2,1)S(1)}, u32[]{:S(2)}, u32[]{:S(2)}) async-start(bf16[8,2,128,256]{2,3,1,0:T(8,128)(2,1)} %bitcast.98), calls=%async_computation.2 | async-start | bytes 2097152 | tf_op jit(solution)/shard_map/all_to_all | solution.py:106
  161.9 0.9 multiply_reduce_fusion
  162.8 28.2 %all-to-all-done.2 = bf16[8,2,128,256]{2,3,1,0:T(8,128)(2,1)S(1)} async-done(((bf16[8,2,128,256]{2,3,1,0:T(8,128)(2,1)}), bf16[8,2,128,256]{2,3,1,0:T(8,128)(2,1)S(1)}, u32[]{:S(2)}, u32[]{:S(2)}) %all-to-all-start.2) | async-done | bytes 1048608 | tf_op jit(solution)/shard_map/all_to_all | solution.py:106
  190.9 4.3 %all-to-all-start.4 = ((bf16[32,8,256]{2,1,0:T(8,128)(2,1)}), bf16[32,8,256]{2,1,0:T(8,128)(2,1)S(1)}, u32[]{:S(2)}, u32[]{:S(2)}) async-start(bf16[32,8,256]{2,1,0:T(8,128)(2,1)} %multiply_reduce_fusion), calls=%async_computation.4 | async-start | bytes 262144 | tf_op jit(solution)/shard_map/all_to_all | solution.py:95
  195.3 0.9 copy.195
  196.6 1.2 copy.171
  197.9 5.0 %all-to-all-done.4 = bf16[32,8,256]{2,1,0:T(8,128)(2,1)S(1)} async-done(((bf16[32,8,256]{2,1,0:T(8,128)(2,1)}), bf16[32,8,256]{2,1,0:T(8,128)(2,1)S(1)}, u32[]{:S(2)}, u32[]{:S(2)}) %all-to-all-start.4) | async-done | bytes 131104 | tf_op jit(solution)/shard_map/all_to_all | solution.py:95
  202.9 1.4 fusion.4
  (75 shorter events, 6.1 us)
Async XLA Ops:
  0.6 112.9 %copy-start = (bf16[256,256]{1,0:T(8,128)(2,1)S(1)}, bf16[256,256]{1,0:T(8,128)(2,1)}, u32[]{:S(2)}) copy-start(bf16[256,256]{1,0:T(8,128)(2,1)} %param.13) | copy-start | bytes 393220
  0.6 50.1 %copy-start.1 = (bf16[2048,256]{1,0:T(8,128)(2,1)S(1)}, bf16[2048,256]{1,0:T(8,128)(2,1)}, u32[]{:S(2)}) copy-start(bf16[2048,256]{1,0:T(8,128)(2,1)} %param.11) | copy-start | bytes 3145732
  2.3 59.8 %all-to-all-start.1 = ((bf16[32,8,256]{2,1,0:T(8,128)(2,1)}), bf16[32,8,256]{2,1,0:T(8,128)(2,1)S(1)}, u32[]{:S(2)}, u32[]{:S(2)}) async-start(bf16[32,8,256]{2,1,0:T(8,128)(2,1)} %slice_bitcast_fusion.13), calls=%async_computation.1 | async-start | bytes 262144 | tf_op jit(solution)/shard_map/all_to_all | solution.py:31
  43.1 9.2 %copy-start.12 = (s32[1,8]{1,0:T(1,128)S(1)}, s32[1,8]{1,0:T(1,128)}, u32[]{:S(2)}) copy-start(s32[1,8]{1,0:T(1,128)} %param.18) | copy-start | bytes 100
  43.1 9.3 %copy-start.2 = (bf16[1,8,2,128,128]{4,3,2,1,0:T(8,128)(2,1)S(1)}, bf16[1,8,2,128,128]{4,3,2,1,0:T(8,128)(2,1)}, u32[]{:S(2)}) copy-start(bf16[1,8,2,128,128]{4,3,2,1,0:T(8,128)(2,1)} %param.20) | copy-start | bytes 1572868
  52.4 9.6 %copy-start.10 = (f32[16]{0:T(128)}, f32[16]{0:T(128)S(1)}, u32[]{:S(2)}) copy-start(f32[16]{0:T(128)S(1)} %reshape.208) | copy-start | bytes 196
  52.6 3.7 %copy-start.7 = (bf16[256,256]{1,0:T(8,128)(2,1)S(1)}, bf16[256,256]{1,0:T(8,128)(2,1)}, u32[]{:S(2)}) copy-start(bf16[256,256]{1,0:T(8,128)(2,1)} %param.12) | copy-start | bytes 393220
  62.2 37.6 %slice-start = ((s8[6291456]{0:T(1024)(128)(4,1)}), s8[2097152]{0:T(1024)(128)(4,1)S(1)}, s32[]{:S(2)}) async-start(s8[6291456]{0:T(1024)(128)(4,1)} %bitcast.265), calls=%async_computation.5 | async-start | bytes 4194304
  62.2 40.4 %all-to-all-start = ((bf16[8,2,128,256]{2,3,1,0:T(8,128)(2,1)}), bf16[8,2,128,256]{2,3,1,0:T(8,128)(2,1)}, u32[]{:S(2)}, u32[]{:S(2)}) async-start(bf16[8,2,128,256]{2,3,1,0:T(8,128)(2,1)} %copy.133), calls=%async_computation | async-start | bytes 2097152 | tf_op jit(solution)/shard_map/all_to_all | solution.py:46
  96.1 3.6 %slice-start.1 = ((s8[6291456]{0:T(1024)(128)(4,1)}), s8[4194304]{0:T(1024)(128)(4,1)S(1)}, s32[]{:S(2)}) async-start(s8[6291456]{0:T(1024)(128)(4,1)} %bitcast.265), calls=%async_computation.6 | async-start | bytes 8388608
  111.6 1.9 copy-start.13
  119.5 1.0 copy-start.3
  120.4 12.4 %copy-start.5 = (bf16[2048,256]{0,1:T(8,128)(2,1)}, bf16[2048,256]{0,1:T(8,128)(2,1)S(1)}, u32[]{:S(2)}) copy-start(bf16[2048,256]{0,1:T(8,128)(2,1)S(1)} %fusion.5) | copy-start | bytes 3145732
  135.3 8.7 %copy-start.6 = (bf16[2048,256]{0,1:T(8,128)(2,1)S(1)}, bf16[2048,256]{0,1:T(8,128)(2,1)}, u32[]{:S(2)}) copy-start(bf16[2048,256]{0,1:T(8,128)(2,1)} %copy-done.5) | copy-start | bytes 3145732
  135.3 9.2 %copy-start.11 = (f32[16]{0:T(128)S(1)}, f32[16]{0:T(128)}, u32[]{:S(2)}) copy-start(f32[16]{0:T(128)} %copy-done.10) | copy-start | bytes 196
  135.3 19.5 %all-to-all-start.3 = ((bf16[6,32,8,256]{3,2,0,1:T(8,128)(2,1)}), bf16[6,32,8,256]{3,2,0,1:T(8,128)(2,1)S(1)}, u32[]{:S(2)}, u32[]{:S(2)}) async-start(bf16[6,32,8,256]{3,2,0,1:T(8,128)(2,1)} %fusion.19), calls=%async_computation.3 | async-start | bytes 1572864 | tf_op jit(solution)/shard_map/all_to_all | solution.py:90
  144.5 17.2 %copy-start.9 = (s32[6]{0:T(128)S(1)}, s32[6]{0:T(128)}, u32[]{:S(2)}) copy-start(s32[6]{0:T(128)} %param.15) | copy-start | bytes 76
  154.8 36.2 %all-to-all-start.2 = ((bf16[8,2,128,256]{2,3,1,0:T(8,128)(2,1)}), bf16[8,2,128,256]{2,3,1,0:T(8,128)(2,1)S(1)}, u32[]{:S(2)}, u32[]{:S(2)}) async-start(bf16[8,2,128,256]{2,3,1,0:T(8,128)(2,1)} %bitcast.98), calls=%async_computation.2 | async-start | bytes 2097152 | tf_op jit(solution)/shard_map/all_to_all | solution.py:106
  190.9 12.0 %all-to-all-start.4 = ((bf16[32,8,256]{2,1,0:T(8,128)(2,1)}), bf16[32,8,256]{2,1,0:T(8,128)(2,1)S(1)}, u32[]{:S(2)}, u32[]{:S(2)}) async-start(bf16[32,8,256]{2,1,0:T(8,128)(2,1)} %multiply_reduce_fusion), calls=%async_computation.4 | async-start | bytes 262144 | tf_op jit(solution)/shard_map/all_to_all | solution.py:95
  196.6 6.3 %copy-start.4 = (bf16[2048,256]{1,0:T(8,128)(2,1)S(1)}, bf16[2048,256]{1,0:T(8,128)(2,1)}, u32[]{:S(2)}) copy-start(bf16[2048,256]{1,0:T(8,128)(2,1)} %copy-done.3) | copy-start | bytes 3145732
  196.6 6.3 %copy-start.8 = (bf16[256,256]{1,0:T(8,128)(2,1)S(1)}, bf16[256,256]{1,0:T(8,128)(2,1)}, u32[]{:S(2)}) copy-start(bf16[256,256]{1,0:T(8,128)(2,1)} %param.12) | copy-start | bytes 393220

commit v2 on v0

v2 whole, which is shorter than its diff:
```python
import functools

import jax
import jax.numpy as jnp
from jax import lax
from jax.experimental import pallas as pl
from jax.experimental.pallas import tpu as pltpu
from jax.sharding import PartitionSpec as P

MESH = pl.DeviceIdType.MESH
F32 = jnp.float32
BF16 = jnp.bfloat16
CHUNK = 512
NT = (((1,), (1,)), ((), ()))


def offsets(n):
    return sorted(range(1, n), key=lambda d: min(d, n - d))


def dot(a, b):
    return jnp.dot(a, b, preferred_element_type=F32)


def layer_kernel(
    n_row,
    n_col,
    send_ref,
    count_ref,
    dest_ref,
    hub_ref,
    ws,
    wn,
    bias,
    feat_hbm,
    hadj_hbm,
    radj_hbm,
    cot_hbm,
    out_hbm,
    fg_hbm,
    fv,
    hv,
    av,
    avt,
    cv,
    ov,
    gv,
    agv,
    agt,
    fgv,
    pre,
    hs,
    rd,
    outb,
    inc,
    retb,
    rin,
    relf,
    relb,
    chain,
    dchain,
    back,
    a_in,
    b_in,
    sel,
    hb,
    ps,
    sb,
    rs,
    rl,
    ow,
    osib,
    bk,
    bl,
    landed,
    prev_f,
    last_f,
    owned,
    prev_b,
    last_b,
    loc_sem,
    zf_s,
    zf_r,
    zb_s,
    zb_r,
    rf_s,
    rf_r,
    rb_s,
    rb_r,
    a_s,
    a_r,
    g_s,
    g_r,
    c_s,
    c_r,
    d_s,
    d_r,
    sib_s,
    sib_r,
):
    row = lax.axis_index("row")
    col = lax.axis_index("col")
    chip = row // 2
    core = lax.rem(row, 2)
    sib = chip * 2 + 1 - core
    chips = n_row // 2
    nodes, width = ov.shape
    sections, hub_rows = hv.shape[0], hv.shape[2]
    slots, tile = av.shape[1], av.shape[2]
    tiles = nodes // tile
    part = hub_rows // chips
    half = width // 2
    order = offsets(n_col)
    opposite = n_col // 2
    step = opposite // 2
    ways = (step, n_col - step)
    total = slots * n_col
    chunks = nodes // CHUNK
    per = CHUNK // tile
    mine = pl.ds(pl.multiple_of(core * half, half), half)
    other = pl.ds(pl.multiple_of((1 - core) * half, half), half)
    own_part = pl.ds(pl.multiple_of(chip * part, part), part)

    def tile_rows(t):
        return pl.ds(pl.multiple_of(t * tile, tile), tile)

    def chunk_rows(c):
        return pl.ds(pl.multiple_of(c * CHUNK, CHUNK), CHUNK)

    def tiles_of(ref, c):
        return jnp.concatenate([ref[c * per + t] for t in range(per)], axis=0)

    def loop(n, body, start=0):
        def run(i, carry):
            body(i)
            return carry

        lax.fori_loop(start, n, run, 0)

    def remote(src, dst, send, recv, to):
        return pltpu.make_async_remote_copy(
            src_ref=src, dst_ref=dst, send_sem=send, recv_sem=recv, device_id=to, device_id_type=MESH
        )

    def to_col(d):
        return (row, lax.rem(col + d, n_col))

    def chip_of(d):
        return lax.rem(chip + d, chips)

    def to_chip(d):
        return (chip_of(d) * 2 + core, col)

    def part_of(j):
        return pl.ds(pl.multiple_of(j * part, part), part)

    barrier = pltpu.get_barrier_semaphore()
    for d in order:
        pl.semaphore_signal(barrier, inc=1, device_id=to_col(d), device_id_type=MESH)

    def greet(d):
        pl.semaphore_signal(barrier, inc=1, device_id=to_chip(d), device_id_type=MESH)

    loop(chips, greet, 1)
    pl.semaphore_signal(barrier, inc=1, device_id=(sib, col), device_id_type=MESH)

    load_f = pltpu.make_async_copy(feat_hbm, fv, loc_sem.at[0])
    load_a = pltpu.make_async_copy(radj_hbm, av, loc_sem.at[1])
    load_h = pltpu.make_async_copy(hadj_hbm, hv, loc_sem.at[2])
    load_c = pltpu.make_async_copy(cot_hbm, cv, loc_sem.at[3])
    load_f.start()
    load_a.start()
    load_h.start()
    load_c.start()
    load_f.wait()

    def stage(i, d):
        to = lax.rem(col + d, n_col)
        for k in range(slots):
            outb[i, k] = fv[send_ref[to * slots + k]]

    stage(0, order[0])
    stage(len(order) - 1, order[-1])
    pl.semaphore_wait(barrier, n_col - 1 + chips - 1 + 1)

    def ring(buf, land, send, recv, sign):
        copies = {}
        for i, d in enumerate(order):
            to = d if sign > 0 else n_col - d
            if d != opposite:
                copies[i] = remote(buf.at[i], land.at[i], send.at[i, 0], recv.at[i, 0], to_col(to))
        return copies

    def relay_first(buf, rel, send, recv):
        i = len(order) - 1
        return [
            remote(buf.at[i, k], rel.at[k], send.at[k], recv.at[k], to_col(ways[k]))
            for k in range(slots)
        ]

    def relay_second(rel, land, send, recv):
        i = len(order) - 1
        return [
            remote(rel.at[k], land.at[i, k], send.at[i, k], recv.at[i, k], to_col(ways[k]))
            for k in range(slots)
        ]

    fwd = ring(outb, inc, zf_s, zf_r, 1)
    fwd1 = relay_first(outb, relf, rf_s, rf_r)
    fwd2 = relay_second(relf, inc, zf_s, zf_r)
    for c in fwd1:
        c.start()
    fwd[0].start()

    per_tile = tile // part

    def hub_of(j):
        return fv.at[j // per_tile, part_of(lax.rem(j, per_tile)), :]

    def hub_a(d):
        return remote(hub_of(chip_of(d)), a_in.at[chip], a_s.at[d], a_r.at[d], to_chip(d))

    loop(chips, lambda d: hub_a(d).start(), 1)
    a_in[chip] = fv[chip // per_tile, part_of(lax.rem(chip, per_tile)), :]
    for i in range(1, len(order) - 1):
        stage(i, order[i])
        fwd[i].start()

    def self_part(c):
        rows = chunk_rows(c)
        pre[rows, :] = dot(tiles_of(fv, c), ws[...]) + bias[...]

    loop(chunks, self_part)

    loop(chips, lambda d: hub_a(d).wait_recv(), 1)
    swap_b = remote(a_in.at[:, :, other], b_in, sib_s.at[0], sib_r.at[0], (sib, col))
    swap_b.start()

    def source(s):
        d = ([0] + order)[s // slots]
        return lax.rem(col + n_col - d, n_col) * slots + s % slots

    def target(s):
        d = ([0] + order)[s // slots]
        return lax.rem(col + d, n_col) * slots + s % slots

    def is_live(s):
        d = ([0] + order)[s // slots]
        return (s % slots) < count_ref[lax.rem(col + n_col - d, n_col)]

    for s in range(total):
        landed[s] = jnp.where(is_live(s), dest_ref[source(s)], -1)
        owned[s] = send_ref[target(s)]

    def link(keys, prev, last):
        def before(s):
            key = keys[s]
            found = total
            for t in range(total):
                found = jnp.where((t < s) & (keys[t] == key), t, found)
            prev[s] = found

        def final(n):
            found = total
            for t in range(total):
                found = jnp.where(keys[t] == n, t, found)
            last[n] = found

        loop(total, before)
        loop(tiles, final)

    link(landed, prev_f, last_f)
    link(owned, prev_b, last_b)
    chain[total] = jnp.zeros((tile, width), F32)
    back[total] = jnp.zeros((tile, width), F32)
    dchain[total] = jnp.zeros((tile, tile), F32)

    swap_b.wait_recv()
    for s in range(sections):
        h = hub_ref[s]
        h_chip = h // 2
        h_core = h - 2 * h_chip
        both = a_in[h_chip].astype(F32)
        same = jnp.where(core == 0, both[:, :half], both[:, half:])
        across = b_in[h_chip].astype(F32)
        sel[s] = jnp.where(h_core == core, same, across).astype(BF16)
    spread = hb.at[:, own_part, mine]

    def hub_g(d):
        return remote(sel, spread, g_s.at[d], g_r.at[d], to_chip(d))

    loop(chips, lambda d: hub_g(d).start(), 1)
    for s in range(sections):
        hb[s, own_part, mine] = sel[s]

    load_a.wait()
    ones_t = jnp.ones((tile, tile), BF16)

    def weights(s):
        d = ([0] + order)[s // slots]
        return lax.rem(col + n_col - d, n_col), s % slots

    for s in range(total):
        p, k = weights(s)
        w = av[p, k]
        dchain[s] = dot(w, ones_t) + dchain[prev_f[s]]
        avt[s] = w.astype(F32).T.astype(BF16)

    for c in range(slots):
        fwd1[c].wait_recv()
        fwd2[c].start()

    load_h.wait()
    ones_h = jnp.ones((hub_rows, half), BF16)

    def degrees(c):
        rows = chunk_rows(c)
        deg = 1.0 + jnp.concatenate([dchain[last_f[c * per + t]] for t in range(per)], axis=0)
        for s in range(sections):
            deg = deg + dot(hv[s, rows, :], ones_h)
        rd[rows, :] = 1.0 / deg

    loop(chunks, degrees)

    loop(chips, lambda d: hub_g(d).wait_recv(), 1)
    swap_h = remote(hb.at[:, :, mine], hb.at[:, :, mine], sib_s.at[1], sib_r.at[1], (sib, col))
    swap_h.start()
    swap_h.wait_recv()

    def hub_sum(c):
        rows = chunk_rows(c)
        acc = dot(hv[0, rows, :], hb[0])
        for s in range(1, sections):
            acc = acc + dot(hv[s, rows, :], hb[s])
        hs[rows, :] = acc

    loop(chunks, hub_sum)

    for s in range(total):
        i, k = s // slots - 1, s % slots
        p, _ = weights(s)
        if i < 0:
            arrived = fv[send_ref[target(s)]]
        else:
            if order[i] == opposite:
                fwd2[k].wait_recv()
            elif k == 0:
                fwd[i].wait_recv()
            arrived = inc[i, k]
        chain[s] = dot(av[p, k], arrived) + chain[prev_f[s]]
    load_c.wait()

    def middle(c):
        rows = chunk_rows(c)
        raw = hs[rows, :] + jnp.concatenate(
            [chain[last_f[c * per + t]] for t in range(per)], axis=0
        )
        inv = jnp.concatenate([rd[rows, :]] * (width // half), axis=1)
        agg = (raw * inv).astype(BF16)
        x = pre[rows, :] + dot(agg, wn[...])
        sig = 0.5 * jnp.tanh(0.5 * x) + 0.5
        ov[rows, :] = (x * sig).astype(BF16)
        grad = (cv[rows, :].astype(F32) * sig * (1.0 + x * (1.0 - sig))).astype(BF16)
        gv[rows, :] = grad
        back_grad = lax.dot_general(grad, wn[...], NT, preferred_element_type=F32)
        scaled = (back_grad * inv).astype(BF16)
        for t in range(per):
            agv[c * per + t] = scaled[t * tile : (t + 1) * tile]

    loop(chunks, middle)

    def slot_grad(s):
        rows = agv[dest_ref[source(s)]]
        value = jnp.where(is_live(s), dot(avt[s], rows), 0.0)
        return value.astype(BF16)

    bwd = ring(retb, rin, zb_s, zb_r, -1)
    bwd1 = relay_first(retb, relb, rb_s, rb_r)
    bwd2 = relay_second(relb, rin, zb_s, zb_r)
    for i in [len(order) - 1] + list(range(len(order) - 1)):
        for k in range(slots):
            retb[i, k] = slot_grad((i + 1) * slots + k)
        if order[i] == opposite:
            for c in bwd1:
                c.start()
        else:
            bwd[i].start()
    for k in range(slots):
        back[k] = slot_grad(k).astype(F32) + back[prev_b[k]]

    store_o = pltpu.make_async_copy(ov, out_hbm, loc_sem.at[4])
    store_o.start()

    def turn(c):
        agt[:, chunk_rows(c)] = tiles_of(agv, c).astype(F32).T.astype(BF16)

    loop(chunks, turn)

    def hub_part(s):
        value = dot(agt[...], hv[s])
        ps[0, s] = value[:, :half]
        ps[1, s] = value[:, half:]

    loop(sections, hub_part)
    swap_p = remote(ps.at[1 - core], sb, sib_s.at[2], sib_r.at[2], (sib, col))
    swap_p.start()

    def self_grad(c):
        rows = chunk_rows(c)
        pre[rows, :] = lax.dot_general(gv[rows, :], ws[...], NT, preferred_element_type=F32)

    loop(chunks, self_grad)
    swap_p.wait_recv()

    def pair(s):
        rs[s] = (ps[core, s] + sb[s]).astype(BF16)

    loop(sections, pair)

    def hub_c(d):
        return remote(rs.at[:, part_of(chip_of(d)), :], rl.at[chip], c_s.at[d], c_r.at[d], to_chip(d))

    loop(chips, lambda d: hub_c(d).start(), 1)
    for s in range(sections):
        rl[chip, s] = rs[s, own_part, :]
    for c in range(slots):
        bwd1[c].wait_recv()
        bwd2[c].start()
    loop(chips, lambda d: hub_c(d).wait_recv(), 1)
    tot = [rl[0, s].astype(F32) for s in range(sections)]
    for j in range(1, chips):
        tot = [tot[s] + rl[j, s].astype(F32) for s in range(sections)]

    def owners(j):
        for b in range(2):
            value = jnp.zeros((part, half), F32)
            for s in range(sections):
                value = value + jnp.where(hub_ref[s] == j * 2 + b, tot[s], 0.0)
            ow[b, j] = value

    loop(chips, owners)
    swap_o = remote(ow.at[1 - core], osib, sib_s.at[3], sib_r.at[3], (sib, col))
    swap_o.start()
    swap_o.wait_recv()

    def owner_rows(j):
        same = ow[core, j]
        across = osib[j]
        bk[j] = jnp.concatenate(
            [jnp.where(core == 0, same, across), jnp.where(core == 0, across, same)], axis=1
        )

    loop(chips, owner_rows)

    def hub_d(d):
        return remote(bk.at[chip_of(d)], bl.at[own_part, :], d_s.at[d], d_r.at[d], to_chip(d))

    loop(chips, lambda d: hub_d(d).start(), 1)
    bl[own_part, :] = bk[chip]
    loop(chips, lambda d: hub_d(d).wait_recv(), 1)
    pre[pl.ds(0, hub_rows), :] += bl[...].T

    for s in range(slots, total):
        i, k = s // slots - 1, s % slots
        if order[i] == opposite:
            bwd2[k].wait_recv()
        elif k == 0:
            bwd[i].wait_recv()
        back[s] = rin[i, k].astype(F32) + back[prev_b[s]]

    def finish(n):
        rows = tile_rows(n)
        fgv[rows, :] = (pre[rows, :] + back[last_b[n]]).astype(BF16)

    loop(tiles, finish)
    store_g = pltpu.make_async_copy(fgv, fg_hbm, loc_sem.at[5])
    store_g.start()

    for c in list(fwd.values()) + fwd1 + fwd2 + list(bwd.values()) + bwd1 + bwd2:
        c.wait_send()
    for c in (swap_b, swap_h, swap_p, swap_o):
        c.wait_send()
    loop(chips, lambda d: hub_a(d).wait_send(), 1)
    loop(chips, lambda d: hub_g(d).wait_send(), 1)
    loop(chips, lambda d: hub_c(d).wait_send(), 1)
    loop(chips, lambda d: hub_d(d).wait_send(), 1)
    store_o.wait()
    store_g.wait()


def shards(
    features,
    w_self,
    w_neigh,
    bias,
    hub_ids,
    hub_adj,
    send_tile,
    recv_count,
    recv_dst,
    recv_adj,
    cotangent,
):
    n_row, n_col = lax.axis_size("row"), lax.axis_size("col")
    nodes, width = features.shape
    sections, hub_rows = hub_adj.shape[1], hub_adj.shape[3]
    peers, slots, tile = recv_adj.shape[1:4]
    total = peers * slots
    tiles = nodes // tile
    chips = n_row // 2
    part = hub_rows // chips
    half = width // 2
    others = n_col - 1
    vmem, smem, dma = pltpu.VMEM, pltpu.SMEM, pltpu.SemaphoreType.DMA
    spec = lambda space: pl.BlockSpec(memory_space=space)
    return pl.pallas_call(
        functools.partial(layer_kernel, n_row, n_col),
        out_shape=(
            jax.ShapeDtypeStruct((nodes, width), BF16),
            jax.ShapeDtypeStruct((nodes, width), BF16),
        ),
        in_specs=[spec(smem)] * 4 + [spec(vmem)] * 3 + [spec(pl.ANY)] * 4,
        out_specs=(spec(pl.ANY), spec(pl.ANY)),
        scratch_shapes=[
            vmem((tiles, tile, width), BF16),
            vmem((sections, nodes, hub_rows), BF16),
            vmem((peers, slots, tile, tile), BF16),
            vmem((total, tile, tile), BF16),
            vmem((nodes, width), BF16),
            vmem((nodes, width), BF16),
            vmem((nodes, width), BF16),
            vmem((tiles, tile, width), BF16),
            vmem((width, nodes), BF16),
            vmem((nodes, width), BF16),
            vmem((nodes, width), F32),
            vmem((nodes, width), F32),
            vmem((nodes, half), F32),
            vmem((others, slots, tile, width), BF16),
            vmem((others, slots, tile, width), BF16),
            vmem((others, slots, tile, width), BF16),
            vmem((others, slots, tile, width), BF16),
            vmem((slots, tile, width), BF16),
            vmem((slots, tile, width), BF16),
            vmem((total + 1, tile, width), F32),
            vmem((total + 1, tile, tile), F32),
            vmem((total + 1, tile, width), F32),
            vmem((chips, part, width), BF16),
            vmem((chips, part, half), BF16),
            vmem((sections, part, half), BF16),
            vmem((sections, hub_rows, width), BF16),
            vmem((2, sections, width, half), F32),
            vmem((sections, width, half), F32),
            vmem((sections, width, half), BF16),
            vmem((chips, sections, part, half), BF16),
            vmem((2, chips, part, half), F32),
            vmem((chips, part, half), F32),
            vmem((chips, part, width), F32),
            vmem((hub_rows, width), F32),
            smem((total,), jnp.int32),
            smem((total,), jnp.int32),
            smem((tiles,), jnp.int32),
            smem((total,), jnp.int32),
            smem((total,), jnp.int32),
            smem((tiles,), jnp.int32),
            dma((6,)),
            dma((others, slots)),
            dma((others, slots)),
            dma((others, slots)),
            dma((others, slots)),
            dma((slots,)),
            dma((slots,)),
            dma((slots,)),
            dma((slots,)),
            dma((chips,)),
            dma((chips,)),
            dma((chips,)),
            dma((chips,)),
            dma((chips,)),
            dma((chips,)),
            dma((chips,)),
            dma((chips,)),
            dma((4,)),
            dma((4,)),
        ],
        compiler_params=pltpu.CompilerParams(
            collective_id=0, has_side_effects=True, vmem_limit_bytes=52 * 2**20
        ),
        name="layer",
    )(
        send_tile.reshape(total),
        recv_count.reshape(peers),
        recv_dst.reshape(total),
        hub_ids,
        w_self,
        w_neigh,
        bias.reshape(1, width),
        features.reshape(tiles, tile, width),
        hub_adj.reshape(hub_adj.shape[1:]),
        recv_adj.reshape(recv_adj.shape[1:]),
        cotangent,
    )


def solution(mesh):
    placed = (
        P(("row", "col"), None),
        P(),
        P(),
        P(),
        P(),
        P(("row", "col"), None, None, None),
        P(("row", "col"), None, None),
        P(("row", "col"), None),
        P(("row", "col"), None, None),
        P(("row", "col"), None, None, None, None),
        P(("row", "col"), None),
    )
    return jax.shard_map(
        shards,
        mesh=mesh,
        in_specs=placed,
        out_specs=(P(("row", "col"), None), P(("row", "col"), None)),
        check_vma=False,
    )
```

time: 320 us -> 75 us (0.23)
  waiting for transfers between devices: 229 us -> 0 us
  Pallas kernels: 0 us -> 64.3 us
  matrix products: 38.3 us -> 0 us
  between operations: 18.2 us -> 0.65 us
  starting transfers between devices: 16.2 us -> 0 us
  other arithmetic: 5.03 us -> 0 us
  local copies, waits for them, and re-layouts: 13.4 us -> 9.75 us
    psum x2 -> x0, waiting for transfers between devices: 228 us -> none  [the longest x1 117 us: shards(): summed_section = lax.psum(partial_grad, 'row')]
    pallas_call x0 -> x1, Pallas kernels: none -> 64.3 us  [shards(): pl.pallas_call(functools.partial(layer_kernel, n_row, n_col), out_shape=(...]
    dot_general x20 -> x0, matrix products: 38.3 us -> none  [the longest x6 14.7 us: shards(): lax.dot_general(adjacency[section], agg_grad, (((0,), (0,)), ((), ())), p...]
    all_to_all x2 -> x0, starting transfers between devices: 15.9 us -> none  [the longest x1 9.15 us: shards(): lax.all_to_all(outgoing, 'col', split_axis=0, concat_axis=0, tiled=True)]
    unnamed x38 -> x16, local copies, waits for them, and re-layouts: 1.87 us -> 9.58 us
    dot_general x3 -> x0, local copies, waits for them, and re-layouts: 6.02 us -> none  [the longest x1 2.57 us: shards(): jnp.einsum('sn,sid->nid', select, contrib, precision=lax.Precision.HIGHEST)]
    reduce_sum x2 -> x0, other arithmetic: 3.93 us -> none  [the longest x1 3.71 us: shards(): degree = 1.0 + jnp.sum(adjacency.astype(f32), axis=(0, 2)) + tile_deg]
    gather x2 -> x0, local copies, waits for them, and re-layouts: 3.51 us -> none  [the longest x1 2.89 us: shards(): features.reshape(count_tiles, tile, width)[offered]]
  transfers between devices with their start and end apart: 4 -> 0, of which waited for: 2 -> 0; matrix products, arithmetic and copies ran while one was open for 7% -> 0% of each run, Pallas kernels for 0% -> 0%
where the time goes in v2:
time: 75 us; the launch traced here: 74.7 us
  Pallas kernels  64.3 us (86%)
  local copies, waits for them, and re-layouts  9.75 us (13%)
    pallas_call x1, Pallas kernels, shards(): pl.pallas_call(functools.partial(layer_kernel, n_row, n_col), out_shape=(...  64.3 us
    unnamed x16, local copies, waits for them, and re-layouts  9.58 us

profile of v2, /device:TPU:1, one launch (start us, length us, event | category | flops | bytes accessed | tf_op | source)
XLA Modules:
  0.0 74.7 jit_solution(7213422433327558358)
XLA Ops:
  0.6 0.8 %copy.15 = s32[1,8,2]{2,1,0:T(8,128)S(1)} copy(s32[1,8,2]{1,2,0:T(2,128)} %param.17) | data formatting | bytes 128 | tf_op args[6]
  1.4 0.1 reshape.25.send_ref
  1.5 0.8 %copy.16 = s32[1,8,2]{2,1,0:T(8,128)S(1)} copy(s32[1,8,2]{1,2,0:T(2,128)} %param.19) | data formatting | bytes 128 | tf_op args[8]
  2.2 0.1 reshape.27.dest_ref
  2.3 0.0 copy-start
  2.3 1.0 %copy-done = bf16[1,8,2,128,128]{4,3,2,1,0:T(8,128)(2,1)S(1)} copy-done((bf16[1,8,2,128,128]{4,3,2,1,0:T(8,128)(2,1)S(1)}, bf16[1,8,2,128,128]{4,3,2,1,0:T(8,128)(2,1)}, u32[]{:S(2)}) %copy-start) | copy-done | bytes 524312
  3.3 0.0 copy-start.1
  3.4 0.9 %copy-done.1 = bf16[256,256]{1,0:T(8,128)(2,1)S(1)} copy-done((bf16[256,256]{1,0:T(8,128)(2,1)S(1)}, bf16[256,256]{1,0:T(8,128)(2,1)}, u32[]{:S(2)}) %copy-start.1) | copy-done | bytes 131096
  4.3 0.0 copy-start.2
  4.3 0.9 %copy-done.2 = bf16[256,256]{1,0:T(8,128)(2,1)S(1)} copy-done((bf16[256,256]{1,0:T(8,128)(2,1)S(1)}, bf16[256,256]{1,0:T(8,128)(2,1)}, u32[]{:S(2)}) %copy-start.2) | copy-done | bytes 131096
  5.2 0.0 copy-start.3
  5.2 0.7 copy-done.3
  5.8 0.0 copy-start.4
  5.8 0.7 copy-done.4
  6.5 0.0 copy-start.5
  6.5 0.7 copy-done.5
  7.1 64.3 %layer.1 = (bf16[2048,256]{1,0:T(8,128)(2,1)S(1)}, bf16[2048,256]{1,0:T(8,128)(2,1)}) custom-call(s32[16]{0:T(128)S(1)} %reshape.25.send_ref, s32[8]{0:T(128)S(1)} %bitcast.7, s32[16]{0:T(128)S(1)} %reshape.27.dest_ref, s32[6]{0:T(128)S(1)} %copy-done.5, bf16[256,256]{1,0:T(8,128)(2,1)S(1)} %copy-done.1, bf16[256,256]{1,0:T(8,128)(2,1)S(1)} %copy-done.2, ...), custom_call_target="tpu_custom_call" | custom-call | tf_op jit(solution)/shard_map/layer/pallas_call | solution.py:516
  71.5 1.0 %copy.19 = bf16[2048,256]{1,0:T(8,128)(2,1)} copy(bf16[2048,256]{1,0:T(8,128)(2,1)S(1)} %get-tuple-element.4) | data formatting | bytes 2097152
  72.5 2.3 %copy.20 = bf16[2048,256]{1,0:T(8,128)(2,1)} copy(bf16[2048,256]{1,0:T(8,128)(2,1)} %get-tuple-element.5) | data formatting | bytes 2097152
Async XLA Ops:
  2.3 1.0 %copy-start = (bf16[1,8,2,128,128]{4,3,2,1,0:T(8,128)(2,1)S(1)}, bf16[1,8,2,128,128]{4,3,2,1,0:T(8,128)(2,1)}, u32[]{:S(2)}) copy-start(bf16[1,8,2,128,128]{4,3,2,1,0:T(8,128)(2,1)} %param.20) | copy-start | bytes 1572868
  3.3 0.9 %copy-start.1 = (bf16[256,256]{1,0:T(8,128)(2,1)S(1)}, bf16[256,256]{1,0:T(8,128)(2,1)}, u32[]{:S(2)}) copy-start(bf16[256,256]{1,0:T(8,128)(2,1)} %ws.1) | copy-start | bytes 393220
  4.3 0.9 %copy-start.2 = (bf16[256,256]{1,0:T(8,128)(2,1)S(1)}, bf16[256,256]{1,0:T(8,128)(2,1)}, u32[]{:S(2)}) copy-start(bf16[256,256]{1,0:T(8,128)(2,1)} %wn.1) | copy-start | bytes 393220
  5.2 0.7 copy-start.3
  5.8 0.7 copy-start.4
  6.5 0.7 copy-start.5

commit v3 on v2

--- a/solution.py
+++ b/solution.py
@@ -11,6 +11,7 @@
 F32 = jnp.float32
 BF16 = jnp.bfloat16
 CHUNK = 512
+PIECES = 4
 NT = (((1,), (1,)), ((), ()))
 
 
@@ -25,6 +26,19 @@
 def layer_kernel(
     n_row,
     n_col,
+    send_hbm,
+    count_hbm,
+    dest_hbm,
+    hub_hbm,
+    ws_hbm,
+    wn_hbm,
+    bias_hbm,
+    feat_hbm,
+    hadj_hbm,
+    radj_hbm,
+    cot_hbm,
+    out_hbm,
+    fg_hbm,
     send_ref,
     count_ref,
     dest_ref,
@@ -32,12 +46,6 @@
     ws,
     wn,
     bias,
-    feat_hbm,
-    hadj_hbm,
-    radj_hbm,
-    cot_hbm,
-    out_hbm,
-    fg_hbm,
     fv,
     hv,
     av,
@@ -55,8 +63,6 @@
     inc,
     retb,
     rin,
-    relf,
-    relb,
     chain,
     dchain,
     back,
@@ -83,10 +89,6 @@
     zf_r,
     zb_s,
     zb_r,
-    rf_s,
-    rf_r,
-    rb_s,
-    rb_r,
     a_s,
     a_r,
     g_s,
@@ -111,9 +113,6 @@
     part = hub_rows // chips
     half = width // 2
     order = offsets(n_col)
-    opposite = n_col // 2
-    step = opposite // 2
-    ways = (step, n_col - step)
     total = slots * n_col
     chunks = nodes // CHUNK
     per = CHUNK // tile
@@ -164,52 +163,40 @@
     loop(chips, greet, 1)
     pl.semaphore_signal(barrier, inc=1, device_id=(sib, col), device_id_type=MESH)
 
-    load_f = pltpu.make_async_copy(feat_hbm, fv, loc_sem.at[0])
-    load_a = pltpu.make_async_copy(radj_hbm, av, loc_sem.at[1])
-    load_h = pltpu.make_async_copy(hadj_hbm, hv, loc_sem.at[2])
-    load_c = pltpu.make_async_copy(cot_hbm, cv, loc_sem.at[3])
-    load_f.start()
-    load_a.start()
-    load_h.start()
-    load_c.start()
-    load_f.wait()
+    pairs = (
+        (send_hbm, send_ref),
+        (feat_hbm, fv),
+        (dest_hbm, dest_ref),
+        (count_hbm, count_ref),
+        (hub_hbm, hub_ref),
+        (ws_hbm, ws),
+        (bias_hbm, bias),
+        (radj_hbm, av),
+        (hadj_hbm, hv),
+        (wn_hbm, wn),
+        (cot_hbm, cv),
+    )
+    loads = [pltpu.make_async_copy(src, dst, loc_sem.at[i]) for i, (src, dst) in enumerate(pairs)]
+    for c in loads:
+        c.start()
+    loads[0].wait()
+    loads[1].wait()
 
     def stage(i, d):
         to = lax.rem(col + d, n_col)
         for k in range(slots):
-            outb[i, k] = fv[send_ref[to * slots + k]]
+            outb[i, k] = fv[send_ref[k, to]]
 
     stage(0, order[0])
-    stage(len(order) - 1, order[-1])
     pl.semaphore_wait(barrier, n_col - 1 + chips - 1 + 1)
 
     def ring(buf, land, send, recv, sign):
-        copies = {}
-        for i, d in enumerate(order):
-            to = d if sign > 0 else n_col - d
-            if d != opposite:
-                copies[i] = remote(buf.at[i], land.at[i], send.at[i, 0], recv.at[i, 0], to_col(to))
-        return copies
-
-    def relay_first(buf, rel, send, recv):
-        i = len(order) - 1
         return [
-            remote(buf.at[i, k], rel.at[k], send.at[k], recv.at[k], to_col(ways[k]))
-            for k in range(slots)
+            remote(buf.at[i], land.at[i], send.at[i], recv.at[i], to_col(d if sign > 0 else n_col - d))
+            for i, d in enumerate(order)
         ]
 
-    def relay_second(rel, land, send, recv):
-        i = len(order) - 1
-        return [
-            remote(rel.at[k], land.at[i, k], send.at[i, k], recv.at[i, k], to_col(ways[k]))
-            for k in range(slots)
-        ]
-
     fwd = ring(outb, inc, zf_s, zf_r, 1)
-    fwd1 = relay_first(outb, relf, rf_s, rf_r)
-    fwd2 = relay_second(relf, inc, zf_s, zf_r)
-    for c in fwd1:
-        c.start()
     fwd[0].start()
 
     per_tile = tile // part
@@ -222,9 +209,12 @@
 
     loop(chips, lambda d: hub_a(d).start(), 1)
     a_in[chip] = fv[chip // per_tile, part_of(lax.rem(chip, per_tile)), :]
-    for i in range(1, len(order) - 1):
+    for i in range(1, len(order)):
         stage(i, order[i])
         fwd[i].start()
+
+    loads[5].wait()
+    loads[6].wait()
 
     def self_part(c):
         rows = chunk_rows(c)
@@ -236,21 +226,29 @@
     swap_b = remote(a_in.at[:, :, other], b_in, sib_s.at[0], sib_r.at[0], (sib, col))
     swap_b.start()
 
-    def source(s):
-        d = ([0] + order)[s // slots]
-        return lax.rem(col + n_col - d, n_col) * slots + s % slots
-
-    def target(s):
-        d = ([0] + order)[s // slots]
-        return lax.rem(col + d, n_col) * slots + s % slots
+    for c in loads[2:5]:
+        c.wait()
+
+    def offset(s):
+        return ([0] + order)[s // slots]
+
+    def weights(s):
+        return lax.rem(col + n_col - offset(s), n_col), s % slots
+
+    def landing(s):
+        p, k = weights(s)
+        return dest_ref[k, p]
+
+    def offered(s):
+        return send_ref[s % slots, lax.rem(col + offset(s), n_col)]
 
     def is_live(s):
-        d = ([0] + order)[s // slots]
-        return (s % slots) < count_ref[lax.rem(col + n_col - d, n_col)]
+        p, k = weights(s)
+        return k < count_ref[p]
 
     for s in range(total):
-        landed[s] = jnp.where(is_live(s), dest_ref[source(s)], -1)
-        owned[s] = send_ref[target(s)]
+        landed[s] = jnp.where(is_live(s), landing(s), -1)
+        owned[s] = offered(s)
 
     def link(keys, prev, last):
         def before(s):
@@ -293,12 +291,8 @@
     for s in range(sections):
         hb[s, own_part, mine] = sel[s]
 
-    load_a.wait()
+    loads[7].wait()
     ones_t = jnp.ones((tile, tile), BF16)
-
-    def weights(s):
-        d = ([0] + order)[s // slots]
-        return lax.rem(col + n_col - d, n_col), s % slots
 
     for s in range(total):
         p, k = weights(s)
@@ -306,11 +300,7 @@
         dchain[s] = dot(w, ones_t) + dchain[prev_f[s]]
         avt[s] = w.astype(F32).T.astype(BF16)
 
-    for c in range(slots):
-        fwd1[c].wait_recv()
-        fwd2[c].start()
-
-    load_h.wait()
+    loads[8].wait()
     ones_h = jnp.ones((hub_rows, half), BF16)
 
     def degrees(c):
@@ -340,15 +330,14 @@
         i, k = s // slots - 1, s % slots
         p, _ = weights(s)
         if i < 0:
-            arrived = fv[send_ref[target(s)]]
+            arrived = fv[offered(s)]
         else:
-            if order[i] == opposite:
-                fwd2[k].wait_recv()
-            elif k == 0:
+            if k == 0:
                 fwd[i].wait_recv()
             arrived = inc[i, k]
         chain[s] = dot(av[p, k], arrived) + chain[prev_f[s]]
-    load_c.wait()
+    loads[9].wait()
+    loads[10].wait()
 
     def middle(c):
         rows = chunk_rows(c)
@@ -370,25 +359,19 @@
     loop(chunks, middle)
 
     def slot_grad(s):
-        rows = agv[dest_ref[source(s)]]
+        rows = agv[landing(s)]
         value = jnp.where(is_live(s), dot(avt[s], rows), 0.0)
         return value.astype(BF16)
 
     bwd = ring(retb, rin, zb_s, zb_r, -1)
-    bwd1 = relay_first(retb, relb, rb_s, rb_r)
-    bwd2 = relay_second(relb, rin, zb_s, zb_r)
-    for i in [len(order) - 1] + list(range(len(order) - 1)):
+    for i in range(len(order)):
         for k in range(slots):
             retb[i, k] = slot_grad((i + 1) * slots + k)
-        if order[i] == opposite:
-            for c in bwd1:
-                c.start()
-        else:
-            bwd[i].start()
+        bwd[i].start()
     for k in range(slots):
         back[k] = slot_grad(k).astype(F32) + back[prev_b[k]]
 
-    store_o = pltpu.make_async_copy(ov, out_hbm, loc_sem.at[4])
+    store_o = pltpu.make_async_copy(ov, out_hbm, loc_sem.at[11])
     store_o.start()
 
     def turn(c):
@@ -423,9 +406,6 @@
     loop(chips, lambda d: hub_c(d).start(), 1)
     for s in range(sections):
         rl[chip, s] = rs[s, own_part, :]
-    for c in range(slots):
-        bwd1[c].wait_recv()
-        bwd2[c].start()
     loop(chips, lambda d: hub_c(d).wait_recv(), 1)
     tot = [rl[0, s].astype(F32) for s in range(sections)]
     for j in range(1, chips):
@@ -462,21 +442,20 @@
 
     for s in range(slots, total):
         i, k = s // slots - 1, s % slots
-        if order[i] == opposite:
-            bwd2[k].wait_recv()
-        elif k == 0:
+        if k == 0:
             bwd[i].wait_recv()
         back[s] = rin[i, k].astype(F32) + back[prev_b[s]]
 
-    def finish(n):
-        rows = tile_rows(n)
-        fgv[rows, :] = (pre[rows, :] + back[last_b[n]]).astype(BF16)
-
-    loop(tiles, finish)
-    store_g = pltpu.make_async_copy(fgv, fg_hbm, loc_sem.at[5])
-    store_g.start()
-
-    for c in list(fwd.values()) + fwd1 + fwd2 + list(bwd.values()) + bwd1 + bwd2:
+    store_g = []
+    for c in range(chunks):
+        for t in range(c * per, (c + 1) * per):
+            rows = pl.ds(t * tile, tile)
+            fgv[rows, :] = (pre[rows, :] + back[last_b[t]]).astype(BF16)
+        rows = pl.ds(c * CHUNK, CHUNK)
+        store_g.append(pltpu.make_async_copy(fgv.at[rows, :], fg_hbm.at[rows, :], loc_sem.at[12 + c]))
+        store_g[c].start()
+
+    for c in fwd + bwd:
         c.wait_send()
     for c in (swap_b, swap_h, swap_p, swap_o):
         c.wait_send()
@@ -485,7 +464,25 @@
     loop(chips, lambda d: hub_c(d).wait_send(), 1)
     loop(chips, lambda d: hub_d(d).wait_send(), 1)
     store_o.wait()
-    store_g.wait()
+    for c in store_g:
+        c.wait()
+
+
+def hand_over(a_in, b_in, a_out, b_out, a_buf, b_buf, in_sem, out_sem):
+    size = a_in.shape[0] // PIECES
+    first, second = [], []
+    for n, (src, buf, dst) in enumerate(((a_in, a_buf, a_out), (b_in, b_buf, b_out))):
+        for i in range(PIECES):
+            rows = pl.ds(i * size, size)
+            first.append(pltpu.make_async_copy(src.at[rows, :], buf.at[rows, :], in_sem.at[n, i]))
+            second.append(pltpu.make_async_copy(buf.at[rows, :], dst.at[rows, :], out_sem.at[n, i]))
+    for c in first:
+        c.start()
+    for i, c in enumerate(second):
+        first[i].wait()
+        c.start()
+    for c in second:
+        c.wait()
 
 
 def shards(
@@ -513,15 +510,22 @@
     others = n_col - 1
     vmem, smem, dma = pltpu.VMEM, pltpu.SMEM, pltpu.SemaphoreType.DMA
     spec = lambda space: pl.BlockSpec(memory_space=space)
-    return pl.pallas_call(
+    results = pl.pallas_call(
         functools.partial(layer_kernel, n_row, n_col),
         out_shape=(
             jax.ShapeDtypeStruct((nodes, width), BF16),
             jax.ShapeDtypeStruct((nodes, width), BF16),
         ),
-        in_specs=[spec(smem)] * 4 + [spec(vmem)] * 3 + [spec(pl.ANY)] * 4,
-        out_specs=(spec(pl.ANY), spec(pl.ANY)),
+        in_specs=[spec(pltpu.HBM)] * 11,
+        out_specs=(spec(pltpu.HBM), spec(pltpu.HBM)),
         scratch_shapes=[
+            smem((slots, peers), jnp.int32),
+            smem((peers,), jnp.int32),
+            smem((slots, peers), jnp.int32),
+            smem((sections,), jnp.int32),
+            vmem((width, width), BF16),
+            vmem((width, width), BF16),
+            vmem((1, width), F32),
             vmem((tiles, tile, width), BF16),
             vmem((sections, nodes, hub_rows), BF16),
             vmem((peers, slots, tile, tile), BF16),
@@ -539,8 +543,6 @@
             vmem((others, slots, tile, width), BF16),
             vmem((others, slots, tile, width), BF16),
             vmem((others, slots, tile, width), BF16),
-            vmem((slots, tile, width), BF16),
-            vmem((slots, tile, width), BF16),
             vmem((total + 1, tile, width), F32),
             vmem((total + 1, tile, tile), F32),
             vmem((total + 1, tile, width), F32),
@@ -562,15 +564,11 @@
             smem((total,), jnp.int32),
             smem((total,), jnp.int32),
             smem((tiles,), jnp.int32),
-            dma((6,)),
-            dma((others, slots)),
-            dma((others, slots)),
-            dma((others, slots)),
-            dma((others, slots)),
-            dma((slots,)),
-            dma((slots,)),
-            dma((slots,)),
-            dma((slots,)),
+            dma((12 + nodes // CHUNK,)),
+            dma((others,)),
+            dma((others,)),
+            dma((others,)),
+            dma((others,)),
             dma((chips,)),
             dma((chips,)),
             dma((chips,)),
@@ -583,13 +581,13 @@
             dma((4,)),
         ],
         compiler_params=pltpu.CompilerParams(
-            collective_id=0, has_side_effects=True, vmem_limit_bytes=52 * 2**20
+            collective_id=0, has_side_effects=True, vmem_limit_bytes=60 * 2**20
         ),
         name="layer",
     )(
-        send_tile.reshape(total),
+        send_tile[0].T,
         recv_count.reshape(peers),
-        recv_dst.reshape(total),
+        recv_dst[0].T,
         hub_ids,
         w_self,
         w_neigh,
@@ -599,6 +597,15 @@
         recv_adj.reshape(recv_adj.shape[1:]),
         cotangent,
     )
+    return pl.pallas_call(
+        hand_over,
+        out_shape=[jax.ShapeDtypeStruct((nodes, width), BF16)] * 2,
+        in_specs=[spec(pltpu.HBM)] * 2,
+        out_specs=[spec(pltpu.HBM)] * 2,
+        scratch_shapes=[vmem((nodes, width), BF16)] * 2 + [dma((2, PIECES))] * 2,
+        compiler_params=pltpu.CompilerParams(vmem_limit_bytes=60 * 2**20),
+        name="hand_over",
+    )(*results)
 
 
 def solution(mesh):

time: 75 us -> 65.9 us (0.88)
  local copies, waits for them, and re-layouts: 9.75 us -> 0 us
    unnamed x16 -> x0, local copies, waits for them, and re-layouts: 9.58 us -> none
    pallas_call x0 -> x1, Pallas kernels: none -> 2.4 us  [shards(): pl.pallas_call(hand_over, out_shape=[jax.ShapeDtypeStruct((nodes, width),...]
    pallas_call x1, Pallas kernels: 64.3 us -> 62.6 us  [shards(): pl.pallas_call(functools.partial(layer_kernel, n_row, n_col), out_shape=(...]
where the time goes in v3:
time: 65.9 us; the launch traced here: 65.6 us
  Pallas kernels  65 us (99%)
    pallas_call x1, Pallas kernels, shards(): pl.pallas_call(functools.partial(layer_kernel, n_row, n_col), out_shape=(...  62.6 us
    pallas_call x1, Pallas kernels, shards(): pl.pallas_call(hand_over, out_shape=[jax.ShapeDtypeStruct((nodes, width),...  2.4 us

profile of v3, /device:TPU:1, one launch (start us, length us, event | category | flops | bytes accessed | tf_op | source)
XLA Modules:
  0.0 65.6 jit_solution(1442198330875496426)
XLA Ops:
  0.6 62.6 %layer.1 = (bf16[2048,256]{1,0:T(8,128)(2,1)}, bf16[2048,256]{1,0:T(8,128)(2,1)}) custom-call(s32[2,8]{1,0:T(2,128)} %bitcast.14, s32[8]{0:T(128)} %bitcast.17, s32[2,8]{1,0:T(2,128)} %bitcast.15, s32[6]{0:T(128)} %hub_hbm.1, bf16[256,256]{1,0:T(8,128)(2,1)} %ws_hbm.1, bf16[256,256]{1,0:T(8,128)(2,1)} %wn_hbm.1, f32[1,256]{1,0:T(1,128)} %bitcast.16, ...), custom_call_target="tpu_custom_call" | custom-call | tf_op jit(solution)/shard_map/layer/pallas_call | solution.py:513
  63.2 2.4 %hand_over.1 = (bf16[2048,256]{1,0:T(8,128)(2,1)}, bf16[2048,256]{1,0:T(8,128)(2,1)}) custom-call(bf16[2048,256]{1,0:T(8,128)(2,1)} %get-tuple-element.4.a_in, bf16[2048,256]{1,0:T(8,128)(2,1)} %get-tuple-element.5.b_in), custom_call_target="tpu_custom_call" | custom-call | tf_op jit(solution)/shard_map/hand_over/pallas_call | solution.py:600

commit v4 on v3

--- a/solution.py
+++ b/solution.py
@@ -10,7 +10,10 @@
 MESH = pl.DeviceIdType.MESH
 F32 = jnp.float32
 BF16 = jnp.bfloat16
-CHUNK = 512
+CHUNK = 1024
+OUT_ROWS = 512
+MID = 512
+EARLY = 2
 PIECES = 4
 NT = (((1,), (1,)), ((), ()))
 
@@ -126,8 +129,12 @@
     def chunk_rows(c):
         return pl.ds(pl.multiple_of(c * CHUNK, CHUNK), CHUNK)
 
-    def tiles_of(ref, c):
-        return jnp.concatenate([ref[c * per + t] for t in range(per)], axis=0)
+    def get(ref, first, number):
+        return jnp.concatenate([ref[first + t] for t in range(number)], axis=0)
+
+    def put(ref, first, value):
+        for t in range(value.shape[0] // tile):
+            ref[first + t] = value[t * tile : (t + 1) * tile]
 
     def loop(n, body, start=0):
         def run(i, carry):
@@ -217,8 +224,7 @@
     loads[6].wait()
 
     def self_part(c):
-        rows = chunk_rows(c)
-        pre[rows, :] = dot(tiles_of(fv, c), ws[...]) + bias[...]
+        put(pre, c * per, dot(get(fv, c * per, per), ws[...]) + bias[...])
 
     loop(chunks, self_part)
 
@@ -308,7 +314,7 @@
         deg = 1.0 + jnp.concatenate([dchain[last_f[c * per + t]] for t in range(per)], axis=0)
         for s in range(sections):
             deg = deg + dot(hv[s, rows, :], ones_h)
-        rd[rows, :] = 1.0 / deg
+        put(rd, c * per, 1.0 / deg)
 
     loop(chunks, degrees)
 
@@ -322,7 +328,7 @@
         acc = dot(hv[0, rows, :], hb[0])
         for s in range(1, sections):
             acc = acc + dot(hv[s, rows, :], hb[s])
-        hs[rows, :] = acc
+        put(hs, c * per, acc)
 
     loop(chunks, hub_sum)
 
@@ -339,43 +345,57 @@
     loads[9].wait()
     loads[10].wait()
 
+    def node(raw, inv, own, cot):
+        inv = jnp.concatenate([inv] * (width // half), axis=1)
+        agg = (raw * inv).astype(BF16)
+        x = own + dot(agg, wn[...])
+        sig = 0.5 * jnp.tanh(0.5 * x) + 0.5
+        grad = (cot.astype(F32) * sig * (1.0 + x * (1.0 - sig))).astype(BF16)
+        back_grad = lax.dot_general(grad, wn[...], NT, preferred_element_type=F32)
+        return x * sig, grad, (back_grad * inv).astype(BF16)
+
+    def at_tiles(ns):
+        def pick(ref):
+            return jnp.concatenate([ref[n] for n in ns], axis=0)
+
+        raw = pick(hs) + jnp.concatenate([chain[last_f[n]] for n in ns], axis=0)
+        return node(raw, pick(rd), pick(pre), pick(cv))
+
     def middle(c):
-        rows = chunk_rows(c)
-        raw = hs[rows, :] + jnp.concatenate(
-            [chain[last_f[c * per + t]] for t in range(per)], axis=0
-        )
-        inv = jnp.concatenate([rd[rows, :]] * (width // half), axis=1)
-        agg = (raw * inv).astype(BF16)
-        x = pre[rows, :] + dot(agg, wn[...])
-        sig = 0.5 * jnp.tanh(0.5 * x) + 0.5
-        ov[rows, :] = (x * sig).astype(BF16)
-        grad = (cv[rows, :].astype(F32) * sig * (1.0 + x * (1.0 - sig))).astype(BF16)
+        first = c * (MID // tile)
+        rows = pl.ds(c * MID, MID)
+        value, grad, scaled = at_tiles([first + t for t in range(MID // tile)])
+        ov[rows, :] = value.astype(BF16)
         gv[rows, :] = grad
-        back_grad = lax.dot_general(grad, wn[...], NT, preferred_element_type=F32)
-        scaled = (back_grad * inv).astype(BF16)
-        for t in range(per):
-            agv[c * per + t] = scaled[t * tile : (t + 1) * tile]
-
-    loop(chunks, middle)
-
-    def slot_grad(s):
-        rows = agv[landing(s)]
-        value = jnp.where(is_live(s), dot(avt[s], rows), 0.0)
-        return value.astype(BF16)
+        put(agv, first, scaled)
+
+    def slot_grad(s, rows):
+        return jnp.where(is_live(s), dot(avt[s], rows), 0.0).astype(BF16)
 
     bwd = ring(retb, rin, zb_s, zb_r, -1)
-    for i in range(len(order)):
+    for i in range(EARLY):
+        ready = [(i + 1) * slots + k for k in range(slots)]
+        _, _, rows = at_tiles([landing(s) for s in ready])
+        for k, s in enumerate(ready):
+            retb[i, k] = slot_grad(s, rows[k * tile : (k + 1) * tile])
+        bwd[i].start()
+
+    for c in range(nodes // MID):
+        middle(c)
+
+    for i in range(EARLY, len(order)):
         for k in range(slots):
-            retb[i, k] = slot_grad((i + 1) * slots + k)
+            s = (i + 1) * slots + k
+            retb[i, k] = slot_grad(s, agv[landing(s)])
         bwd[i].start()
     for k in range(slots):
-        back[k] = slot_grad(k).astype(F32) + back[prev_b[k]]
+        back[k] = slot_grad(k, agv[landing(k)]).astype(F32) + back[prev_b[k]]
 
     store_o = pltpu.make_async_copy(ov, out_hbm, loc_sem.at[11])
     store_o.start()
 
     def turn(c):
-        agt[:, chunk_rows(c)] = tiles_of(agv, c).astype(F32).T.astype(BF16)
+        agt[:, chunk_rows(c)] = get(agv, c * per, per).astype(F32).T.astype(BF16)
 
     loop(chunks, turn)
 
@@ -390,7 +410,7 @@
 
     def self_grad(c):
         rows = chunk_rows(c)
-        pre[rows, :] = lax.dot_general(gv[rows, :], ws[...], NT, preferred_element_type=F32)
+        put(pre, c * per, lax.dot_general(gv[rows, :], ws[...], NT, preferred_element_type=F32))
 
     loop(chunks, self_grad)
     swap_p.wait_recv()
@@ -438,7 +458,15 @@
     loop(chips, lambda d: hub_d(d).start(), 1)
     bl[own_part, :] = bk[chip]
     loop(chips, lambda d: hub_d(d).wait_recv(), 1)
-    pre[pl.ds(0, hub_rows), :] += bl[...].T
+    put(pre, 0, get(pre, 0, hub_rows // tile) + bl[...].T)
+
+    for c in fwd:
+        c.wait_send()
+    for c in (swap_b, swap_h, swap_p, swap_o):
+        c.wait_send()
+    for sent in (hub_a, hub_g, hub_c, hub_d):
+        loop(chips, lambda d, sent=sent: sent(d).wait_send(), 1)
+    store_o.wait()
 
     for s in range(slots, total):
         i, k = s // slots - 1, s % slots
@@ -447,23 +475,15 @@
         back[s] = rin[i, k].astype(F32) + back[prev_b[s]]
 
     store_g = []
-    for c in range(chunks):
-        for t in range(c * per, (c + 1) * per):
+    for c in range(nodes // OUT_ROWS):
+        for t in range(c * OUT_ROWS // tile, (c + 1) * OUT_ROWS // tile):
             rows = pl.ds(t * tile, tile)
-            fgv[rows, :] = (pre[rows, :] + back[last_b[t]]).astype(BF16)
-        rows = pl.ds(c * CHUNK, CHUNK)
+            fgv[rows, :] = (pre[t] + back[last_b[t]]).astype(BF16)
+        rows = pl.ds(c * OUT_ROWS, OUT_ROWS)
         store_g.append(pltpu.make_async_copy(fgv.at[rows, :], fg_hbm.at[rows, :], loc_sem.at[12 + c]))
         store_g[c].start()
-
-    for c in fwd + bwd:
+    for c in bwd:
         c.wait_send()
-    for c in (swap_b, swap_h, swap_p, swap_o):
-        c.wait_send()
-    loop(chips, lambda d: hub_a(d).wait_send(), 1)
-    loop(chips, lambda d: hub_g(d).wait_send(), 1)
-    loop(chips, lambda d: hub_c(d).wait_send(), 1)
-    loop(chips, lambda d: hub_d(d).wait_send(), 1)
-    store_o.wait()
     for c in store_g:
         c.wait()
 
@@ -530,15 +550,15 @@
             vmem((sections, nodes, hub_rows), BF16),
             vmem((peers, slots, tile, tile), BF16),
             vmem((total, tile, tile), BF16),
-            vmem((nodes, width), BF16),
+            vmem((tiles, tile, width), BF16),
             vmem((nodes, width), BF16),
             vmem((nodes, width), BF16),
             vmem((tiles, tile, width), BF16),
             vmem((width, nodes), BF16),
             vmem((nodes, width), BF16),
-            vmem((nodes, width), F32),
-            vmem((nodes, width), F32),
-            vmem((nodes, half), F32),
+            vmem((tiles, tile, width), F32),
+            vmem((tiles, tile, width), F32),
+            vmem((tiles, tile, half), F32),
             vmem((others, slots, tile, width), BF16),
             vmem((others, slots, tile, width), BF16),
             vmem((others, slots, tile, width), BF16),
@@ -564,7 +584,7 @@
             smem((total,), jnp.int32),
             smem((total,), jnp.int32),
             smem((tiles,), jnp.int32),
-            dma((12 + nodes // CHUNK,)),
+            dma((12 + nodes // OUT_ROWS,)),
             dma((others,)),
             dma((others,)),
             dma((others,)),
@@ -595,7 +615,7 @@
         features.reshape(tiles, tile, width),
         hub_adj.reshape(hub_adj.shape[1:]),
         recv_adj.reshape(recv_adj.shape[1:]),
-        cotangent,
+        cotangent.reshape(tiles, tile, width),
     )
     return pl.pallas_call(
         hand_over,

time: 65.9 us -> 65.2 us (0.989)
  Pallas kernels: 65 us -> 64.3 us
    pallas_call x1, Pallas kernels: 62.6 us -> 61.9 us  [shards(): pl.pallas_call(functools.partial(layer_kernel, n_row, n_col), out_shape=(...]
where the time goes in v4:
time: 65.2 us; the launch traced here: 65 us
  Pallas kernels  64.3 us (99%)
    pallas_call x1, Pallas kernels, shards(): pl.pallas_call(functools.partial(layer_kernel, n_row, n_col), out_shape=(...  61.9 us
    pallas_call x1, Pallas kernels, shards(): pl.pallas_call(hand_over, out_shape=[jax.ShapeDtypeStruct((nodes, width),...  2.4 us

profile of v4, /device:TPU:1, one launch (start us, length us, event | category | flops | bytes accessed | tf_op | source)
XLA Modules:
  0.0 65.0 jit_solution(8482635079662189230)
XLA Ops:
  0.6 61.9 %layer.1 = (bf16[2048,256]{1,0:T(8,128)(2,1)}, bf16[2048,256]{1,0:T(8,128)(2,1)}) custom-call(s32[2,8]{1,0:T(2,128)} %bitcast.16, s32[8]{0:T(128)} %bitcast.19, s32[2,8]{1,0:T(2,128)} %bitcast.17, s32[6]{0:T(128)} %hub_hbm.1, bf16[256,256]{1,0:T(8,128)(2,1)} %ws_hbm.1, bf16[256,256]{1,0:T(8,128)(2,1)} %wn_hbm.1, f32[1,256]{1,0:T(1,128)} %bitcast.18, ...), custom_call_target="tpu_custom_call" | custom-call | tf_op jit(solution)/shard_map/layer/pallas_call | solution.py:533
  62.6 2.4 %hand_over.1 = (bf16[2048,256]{1,0:T(8,128)(2,1)}, bf16[2048,256]{1,0:T(8,128)(2,1)}) custom-call(bf16[2048,256]{1,0:T(8,128)(2,1)} %get-tuple-element.4.a_in, bf16[2048,256]{1,0:T(8,128)(2,1)} %get-tuple-element.5.b_in), custom_call_target="tpu_custom_call" | custom-call | tf_op jit(solution)/shard_map/hand_over/pallas_call | solution.py:620

commit v5 on v4

--- a/solution.py
+++ b/solution.py
@@ -195,6 +195,7 @@
             outb[i, k] = fv[send_ref[k, to]]
 
     stage(0, order[0])
+    stage(1, order[1])
     pl.semaphore_wait(barrier, n_col - 1 + chips - 1 + 1)
 
     def ring(buf, land, send, recv, sign):
@@ -205,6 +206,7 @@
 
     fwd = ring(outb, inc, zf_s, zf_r, 1)
     fwd[0].start()
+    fwd[1].start()
 
     per_tile = tile // part
 
@@ -216,7 +218,7 @@
 
     loop(chips, lambda d: hub_a(d).start(), 1)
     a_in[chip] = fv[chip // per_tile, part_of(lax.rem(chip, per_tile)), :]
-    for i in range(1, len(order)):
+    for i in range(2, len(order)):
         stage(i, order[i])
         fwd[i].start()
 

time: 65.2 us -> 65.2 us (level)
  no operation moved by 1% of the time
where the time goes in v5:
time: 65.2 us; the launch traced here: 64.9 us
  Pallas kernels  64.3 us (99%)
    pallas_call x1, Pallas kernels, shards(): pl.pallas_call(functools.partial(layer_kernel, n_row, n_col), out_shape=(...  61.9 us
    pallas_call x1, Pallas kernels, shards(): pl.pallas_call(hand_over, out_shape=[jax.ShapeDtypeStruct((nodes, width),...  2.4 us

profile of v5, /device:TPU:1, one launch (start us, length us, event | category | flops | bytes accessed | tf_op | source)
XLA Modules:
  0.0 64.9 jit_solution(9466939347639485277)
XLA Ops:
  0.6 61.9 %layer.1 = (bf16[2048,256]{1,0:T(8,128)(2,1)}, bf16[2048,256]{1,0:T(8,128)(2,1)}) custom-call(s32[2,8]{1,0:T(2,128)} %bitcast.16, s32[8]{0:T(128)} %bitcast.19, s32[2,8]{1,0:T(2,128)} %bitcast.17, s32[6]{0:T(128)} %hub_hbm.1, bf16[256,256]{1,0:T(8,128)(2,1)} %ws_hbm.1, bf16[256,256]{1,0:T(8,128)(2,1)} %wn_hbm.1, f32[1,256]{1,0:T(1,128)} %bitcast.18, ...), custom_call_target="tpu_custom_call" | custom-call | tf_op jit(solution)/shard_map/layer/pallas_call | solution.py:535
  62.5 2.4 %hand_over.1 = (bf16[2048,256]{1,0:T(8,128)(2,1)}, bf16[2048,256]{1,0:T(8,128)(2,1)}) custom-call(bf16[2048,256]{1,0:T(8,128)(2,1)} %get-tuple-element.4.a_in, bf16[2048,256]{1,0:T(8,128)(2,1)} %get-tuple-element.5.b_in), custom_call_target="tpu_custom_call" | custom-call | tf_op jit(solution)/shard_map/hand_over/pallas_call | solution.py:622
